TPU v7x, 32 devices: a whole 2x2x4 slice. The times are simulated.
32 devices in a mesh: groups: 2 (over x), shot: 16 (over z, y, core).
Axes of the slice: x: 2, y: 2, z: 4, core: 2. Of those that a mesh axis runs over, the one named last changes fastest.
Arguments:
- forward_state: float32 [32, 13, 16, 64, 128], P(('groups', 'shot')), parts along dimension 0, may hold values from -6 to 6
- adjoint_state: float32 [32, 13, 16, 64, 128], P(('groups', 'shot')), parts along dimension 0, may hold values from -6 to 6
- source_amp: float32 [32, 2], P(('groups', 'shot')), parts along dimension 0, may hold values from -12 to 12
- source_cell: int32 [32], P(('groups', 'shot')), parts along dimension 0, may hold values from 0 to 131071
- receiver_cells: int32 [32, 1024], P(('groups', 'shot')), parts along dimension 0, may hold values from 0 to 131071
- recorded: float32 [32, 1024], P(('groups', 'shot')), parts along dimension 0, may hold values from -6 to 6
- material: float32 [4, 32, 64, 128], P(None, 'groups', 'shot'), parts along dimension 1, may hold values from 0.3 to 2
- cell_class: int32 [32, 64, 128], P('groups'), parts along dimension 0, may hold values from 0 to 3
- class_factors: float32 [4, 4], replicated, may hold values from 0.5 to 2
Outputs:
- gradient: float32 [4, 32, 64, 128], P(None, 'groups', 'shot'), parts along dimension 1
There are 2 independent parts, one for each index of `groups`. A program takes and returns all parts, laid end to end along the dimension named above; an argument that names none is the same for every part. Nothing has to cross between parts.
All inputs are finite; a program needn't handle non-finite values.
Results may differ from a plain program's by a relative error of at most 0.00002.
Values sent between devices are 32-bit elements; how exact they have to be, the bound alone decides.
No kernel may reach another device: no remote copies, remote signals or barrier semaphores. Data moves between devices by JAX's collectives and lax.ppermute only.
A program may use at most 128 MiB of HBM per device.

v0:
```python
import functools

import jax
import jax.numpy as jnp
from jax import lax
from jax.experimental import pallas as pl
from jax.experimental.pallas import tpu as pltpu
from jax.sharding import PartitionSpec as P

ALPHA = 0.8
RHO_BULK = 2.2
RHO_FLUID = 1.0
MASS_FLUID = 2.5
DT = 0.25
DET = RHO_BULK * MASS_FLUID - RHO_FLUID * RHO_FLUID
C1 = DT * MASS_FLUID / DET
C2 = DT * RHO_FLUID / DET
C3 = DT * RHO_BULK / DET

GUARD = 8
CHUNK = 16
F32 = jnp.float32
BF16 = jnp.bfloat16
PARAMS = pltpu.CompilerParams(vmem_limit_bytes=12 * 1024 * 1024)
SMEM = pl.BlockSpec(memory_space=pltpu.SMEM)
VMEM = pl.BlockSpec(memory_space=pltpu.VMEM)
HBM = pl.BlockSpec(memory_space=pltpu.HBM)

RESIDENT = (
    ("st", 13, True),
    ("q1", 3, True),
    ("q2", 3, True),
    ("eh", 7, True),
    ("fr", 6, True),
    ("adj", 13, False),
    ("hits", 1, False),
    ("seen", 1, False),
    ("strain", 7, False),
    ("model", 4, False),
    ("grad", 4, False),
    ("source", 1, False),
)
NAMES = tuple(name for name, _, _ in RESIDENT)


def in_vmem(x):
    return pltpu.with_memory_space_constraint(x, pltpu.VMEM)


def in_hbm(x):
    return pltpu.with_memory_space_constraint(x, pltpu.HBM)


def cost(cells, ops):
    return pl.CostEstimate(flops=cells * ops, bytes_accessed=cells * 4, transcendentals=0)


def own_kernel(me_ref, class_factors, classes_hbm, material_hbm, factor, *refs):
    *owns, table_ref, classes, material, sems = refs
    _, nx, piece, ny = material.shape
    nx_part = nx // len(owns)
    rows = pl.ds(pl.multiple_of(me_ref[0] * piece, piece), piece)
    table_copy = pltpu.make_async_copy(class_factors, table_ref, sems.at[0])
    class_copy = pltpu.make_async_copy(classes_hbm, classes, sems.at[1])
    material_copy = pltpu.make_async_copy(material_hbm, material, sems.at[2])
    class_copy.start()
    material_copy.start()
    table_copy.start()
    table_copy.wait()
    class_copy.wait()
    material_copy.wait()
    table = [[table_ref[k, c] for c in range(class_factors.shape[1])] for k in range(4)]
    for x in range(nx):
        which = classes[x, rows, :]
        for k in range(4):
            f = jnp.full((piece, ny), table[k][0], F32)
            for c in range(1, len(table[k])):
                f = jnp.where(which == c, table[k][c], f)
            at = (k * nx_part + x % nx_part) * piece
            factor[k, x] = f
            owns[x // nx_part][0, at : at + piece, :] = f * material[k, x]


def own_model(me, class_factors, classes, material, parts):
    _, nx, piece, ny = material.shape
    part = (1, 4 * (nx // parts) * piece, ny)
    return pl.pallas_call(
        own_kernel,
        out_shape=(pltpu.VMEM(material.shape, F32), *[pltpu.VMEM(part, F32)] * parts),
        in_specs=[SMEM, HBM, HBM, HBM],
        out_specs=(VMEM,) * (parts + 1),
        scratch_shapes=[
            pltpu.SMEM(class_factors.shape, F32),
            pltpu.VMEM(classes.shape, jnp.int32),
            pltpu.VMEM(material.shape, F32),
            pltpu.SemaphoreType.DMA((3,)),
        ],
        compiler_params=PARAMS,
        cost_estimate=cost(4 * nx * piece * ny, 10),
        name="own_model",
    )(me, in_hbm(class_factors), in_hbm(classes), in_hbm(material))


def load_kernel(src_cell, amp_hbm, rec_cell_hbm, rec_hbm, state_hbm, adj_hbm, *refs, waits):
    refs = refs[waits:]
    amp_ref, cell_ref, rec_ref, sem_state, sem_adj, sem_small = refs[len(RESIDENT) :]
    r = dict(zip(NAMES, refs))
    nf, nx, nz, ny = state_hbm.shape
    st, adj, hits, seen = r["st"], r["adj"], r["hits"], r["seen"]
    copies = [
        pltpu.make_async_copy(
            state_hbm.at[f], st.at[f, pl.ds(1, nx), pl.ds(GUARD, nz), :], sem_state.at[f]
        )
        for f in range(nf)
    ]
    copies.append(pltpu.make_async_copy(adj_hbm, adj, sem_adj))
    small = [
        pltpu.make_async_copy(src, dst, sem_small.at[i])
        for i, (src, dst) in enumerate(
            ((rec_cell_hbm, cell_ref), (rec_hbm, rec_ref), (amp_hbm, amp_ref))
        )
    ]
    for copy in (*small, *copies):
        copy.start()

    zrow = jnp.zeros((GUARD, ny), F32)
    padded = [(r[name], f) for name, count, pad in RESIDENT if pad for f in range(count)]

    def zero_rows(x, carry):
        for ref, f in padded:
            ref[f, x, 0:GUARD, :] = zrow
            ref[f, x, nz + GUARD : nz + 2 * GUARD, :] = zrow
        return carry

    lax.fori_loop(0, nx + 2, zero_rows, 0)
    for ref, f in padded:
        for x in (0, nx + 1):
            for z in range(GUARD, nz + GUARD, GUARD):
                ref[f, x, z : z + GUARD, :] = zrow

    def zero_source(x, carry):
        r["source"][0, x] = jnp.zeros((nz, ny), F32)
        return carry

    lax.fori_loop(0, nx, zero_source, 0)
    for copy in small:
        copy.wait()

    cell, rec = cell_ref[...], rec_ref[...]
    count = cell.shape[1]
    row = lax.div(cell, ny)
    lane = cell - row * ny
    high = rec.astype(BF16).astype(F32)
    middle = (rec - high).astype(BF16).astype(F32)
    low = rec - high - middle
    match = lax.broadcasted_iota(jnp.int32, (ny, count), 0) == lane
    columns = jnp.concatenate(
        [jnp.where(match, v, 0.0).astype(BF16) for v in (jnp.ones_like(rec), high, middle, low)], 0
    )
    block = 128
    for b in range(0, nx * nz, block):
        rows = lax.broadcasted_iota(jnp.int32, (block, count), 0) + b == row
        out = lax.dot_general(
            jnp.where(rows, 1.0, 0.0).astype(BF16),
            columns,
            (((1,), (1,)), ((), ())),
            preferred_element_type=F32,
        )
        total = out[:, ny : 2 * ny] + out[:, 2 * ny : 3 * ny] + out[:, 3 * ny :]
        for z in range(0, block, nz):
            x = (b + z) // nz
            hits[0, x] = out[z : z + nz, :ny]
            seen[0, x] = total[z : z + nz]

    for copy in copies:
        copy.wait()

    src_x, src_z, src_y = place(src_cell[0], nz, ny)
    here = lax.broadcasted_iota(jnp.int32, (1, ny), 1) == src_y
    at = (src_x, pl.ds(src_z, 1), slice(None))
    r["source"][(0, *at)] = jnp.where(here, amp_ref[0, 0], 0.0)
    adj[(12, *at)] += jnp.where(here, hits[(0, *at)] * amp_ref[0, 1], 0.0)


def place(cell, nz, ny):
    return cell // (nz * ny), (cell // ny) % nz, cell % ny


def load_fields(cell, amps, receivers, recorded, state, adjoint, after):
    nf, nx, nz, ny = state.shape
    shapes = tuple(
        pltpu.VMEM((count, *((nx + 2, nz + 2 * GUARD, ny) if pad else (nx, nz, ny))), F32)
        for _, count, pad in RESIDENT
    )
    return pl.pallas_call(
        functools.partial(load_kernel, waits=len(after)),
        out_shape=shapes,
        in_specs=[SMEM] + [HBM] * 5 + [VMEM] * len(after),
        out_specs=(VMEM,) * len(shapes),
        scratch_shapes=[
            pltpu.SMEM(amps.shape, F32),
            pltpu.VMEM(receivers.shape, jnp.int32),
            pltpu.VMEM(recorded.shape, F32),
            pltpu.SemaphoreType.DMA((nf,)),
            pltpu.SemaphoreType.DMA,
            pltpu.SemaphoreType.DMA((3,)),
        ],
        compiler_params=PARAMS,
        cost_estimate=cost(nx * nz * ny, 150),
        name="load_fields",
    )(
        cell,
        *[in_hbm(x) for x in (amps, receivers, recorded, state, adjoint)],
        *[in_vmem(x) for x in after],
    )


def march_kernel(me_ref, *refs, n, spans, gathered, summed, waits):
    pieces = refs[: 2 * len(gathered)]
    refs = refs[len(pieces) + waits + len(RESIDENT) :]
    r = dict(zip(NAMES, refs))
    outs = refs[len(RESIDENT) :]
    st, q1, q2, eh, fr, adj, hits, seen, strain, model, grad, source = [r[name] for name in NAMES]
    _, nx, nz, ny = adj.shape
    piece = nz // n
    me = me_ref[0]

    def rows_of(rel):
        return pl.ds(pl.multiple_of((me ^ rel) * piece, piece), piece)

    for part, (low, high, rels) in enumerate(gathered):
        span = high - low
        near, core = pieces[2 * part : 2 * part + 2]

        def assemble(x, carry):
            for k in range(4):
                at = pl.ds((k * span + x) * piece, piece)
                for i, rel in enumerate(rels):
                    model[k, low + x, rows_of(rel), :] = near[i, at, :]
                    model[k, low + x, rows_of(rel ^ 1), :] = core[i, at, :]
            return carry

        lax.fori_loop(0, span, assemble, 0)

    lane = lax.broadcasted_iota(jnp.int32, (CHUNK, ny), 1)
    first, last = lane == 0, lane == ny - 1
    zero = jnp.zeros((CHUNK, ny), F32)
    chunk = CHUNK

    def at(ref, f, x, z, dx=0, dz=0):
        return ref[f, x + 1 + dx, pl.ds(GUARD + z + dz, chunk), :]

    def put(ref, f, x, z, value):
        ref[f, x + 1, pl.ds(GUARD + z, chunk), :] = value

    def ahead(f):
        return jnp.where(last, zero, pltpu.roll(f, ny - 1, 1))

    def behind(f):
        return jnp.where(first, zero, pltpu.roll(f, 1, 1))

    def fwd(ref, f, x, z, axis, here=None):
        here = at(ref, f, x, z) if here is None else here
        if axis == 0:
            return at(ref, f, x, z, dx=1) - here
        if axis == 1:
            return at(ref, f, x, z, dz=1) - here
        return ahead(here) - here

    def bwd(ref, f, x, z, axis, here=None):
        here = at(ref, f, x, z) if here is None else here
        if axis == 0:
            return here - at(ref, f, x, z, dx=-1)
        if axis == 1:
            return here - at(ref, f, x, z, dz=-1)
        return here - behind(here)

    def over_cells(number, body):
        begin, end = spans[number]

        def plane(x, carry):
            for z in range(0, nz, chunk):
                body(x, z)
            return carry

        if end > begin:
            lax.fori_loop(begin, end, plane, 0)

    def mod(k, x, z):
        return model[k, x, pl.ds(z, chunk), :]

    def forces(x, z):
        sxx, szz, syy, sxz, sxy, szy, p = [at(st, 6 + i, x, z) for i in range(7)]
        fx = fwd(st, 6, x, z, 0, sxx) + bwd(st, 9, x, z, 1, sxz) + bwd(st, 10, x, z, 2, sxy)
        fz = bwd(st, 9, x, z, 0, sxz) + fwd(st, 7, x, z, 1, szz) + bwd(st, 11, x, z, 2, szy)
        fy = bwd(st, 10, x, z, 0, sxy) + bwd(st, 11, x, z, 1, szy) + fwd(st, 8, x, z, 2, syy)
        g = [fwd(st, 12, x, z, d, p) for d in range(3)]
        return (fx, fz, fy), g

    def velocities(x, z, q_from, q_at, q_to):
        f, g = forces(x, z)
        damp = mod(3, x, z)
        for d in range(3):
            q = at(q_from, q_at + d, x, z)
            drag = g[d] + damp * q
            put(st, d, x, z, at(st, d, x, z) + (C1 * f[d] + C2 * drag))
            put(q_to, d, x, z, q - (C3 * drag + C2 * f[d]))

    def strains(x, z, q):
        vx, vz, vy = [at(st, i, x, z) for i in range(3)]
        exx = bwd(st, 0, x, z, 0, vx)
        ezz = bwd(st, 1, x, z, 1, vz)
        eyy = bwd(st, 2, x, z, 2, vy)
        dq = bwd(q, 0, x, z, 0) + bwd(q, 1, x, z, 1) + bwd(q, 2, x, z, 2)
        hxz = fwd(st, 0, x, z, 1, vx) + fwd(st, 1, x, z, 0, vz)
        hxy = fwd(st, 0, x, z, 2, vx) + fwd(st, 2, x, z, 0, vy)
        hzy = fwd(st, 1, x, z, 2, vz) + fwd(st, 2, x, z, 1, vy)
        dv = exx + ezz + eyy
        w = ALPHA * dv + dq
        return exx, ezz, eyy, hxz, hxy, hzy, dv, w

    def stresses(x, z):
        exx, ezz, eyy, hxz, hxy, hzy, dv, w = strains(x, z, q1)
        lame, shear, biot = [DT * mod(k, x, z) for k in range(3)]
        bw = biot * w
        bulk = lame * dv + ALPHA * bw
        shear2 = 2.0 * shear
        for i, e in enumerate((exx, ezz, eyy)):
            put(st, 6 + i, x, z, at(st, 6 + i, x, z) + (shear2 * e + bulk))
        for i, h in enumerate((hxz, hxy, hzy)):
            put(st, 9 + i, x, z, at(st, 9 + i, x, z) + shear * h)
        put(st, 12, x, z, at(st, 12, x, z) - bw + source[0, x, pl.ds(z, chunk), :])
        for i, e in enumerate((exx, ezz, eyy, hxz, hxy, hzy, w)):
            strain[i, x, pl.ds(z, chunk), :] = e

    def adj_at(f, x, z):
        return adj[f, x, pl.ds(z, chunk), :]

    def correlate(x, z, e, h, w, s, p, first_time):
        lame, shear, biot = [DT * mod(k, x, z) for k in range(3)]
        trace = s[0] + s[1] + s[2]
        dv = e[0] + e[1] + e[2]
        load = ALPHA * trace - p
        diag = s[0] * e[0] + s[1] * e[1] + s[2] * e[2]
        off = s[3] * h[0] + s[4] * h[1] + s[5] * h[2]
        for k, value in enumerate((trace * dv, 2.0 * diag + off, load * w)):
            value = DT * value
            if not first_time:
                value = grad[k, x, pl.ds(z, chunk), :] + value
            grad[k, x, pl.ds(z, chunk), :] = value
        t = biot * load
        bulk = lame * trace + ALPHA * t
        shear2 = 2.0 * shear
        for i in range(3):
            put(eh, i, x, z, shear2 * s[i] + bulk)
        for i in range(3):
            put(eh, 3 + i, x, z, shear * s[3 + i])
        put(eh, 6, x, z, t)

    def stress_back_2(x, z):
        exx, ezz, eyy, hxz, hxy, hzy, dv, w = strains(x, z, q2)
        final_p = at(st, 12, x, z) - DT * mod(2, x, z) * w
        s = [adj_at(6 + i, x, z) for i in range(6)]
        p = adj_at(12, x, z) + (hits[0, x, pl.ds(z, chunk), :] * final_p - seen[0, x, pl.ds(z, chunk), :])
        adj[12, x, pl.ds(z, chunk), :] = p
        correlate(x, z, (exx, ezz, eyy), (hxz, hxy, hzy), w, s, p, True)

    def velocity_bars(x, z, v, q):
        ex, ez, ey, hxz, hxy, hzy, t = [at(eh, i, x, z) for i in range(7)]
        vx = v[0] - (fwd(eh, 0, x, z, 0, ex) + bwd(eh, 3, x, z, 1, hxz) + bwd(eh, 4, x, z, 2, hxy))
        vz = v[1] - (bwd(eh, 3, x, z, 0, hxz) + fwd(eh, 1, x, z, 1, ez) + bwd(eh, 5, x, z, 2, hzy))
        vy = v[2] - (bwd(eh, 4, x, z, 0, hxy) + bwd(eh, 5, x, z, 1, hzy) + fwd(eh, 2, x, z, 2, ey))
        qs = [q[d] - fwd(eh, 6, x, z, d, t) for d in range(3)]
        return (vx, vz, vy), qs

    def velocity_back_2(x, z):
        v, q = velocity_bars(
            x, z, [adj_at(d, x, z) for d in range(3)], [adj_at(3 + d, x, z) for d in range(3)]
        )
        damp = mod(3, x, z)
        total = zero
        for d in range(3):
            r = C3 * q[d] - C2 * v[d]
            put(fr, d, x, z, C1 * v[d] - C2 * q[d])
            put(fr, 3 + d, x, z, r)
            total = total + at(q1, d, x, z) * r
            adj[d, x, pl.ds(z, chunk), :] = v[d]
            adj[3 + d, x, pl.ds(z, chunk), :] = q[d] - damp * r
        grad[3, x, pl.ds(z, chunk), :] = total

    def stress_back_1(x, z):
        fx, fz, fy = [at(fr, i, x, z) for i in range(3)]
        s = [
            adj_at(6, x, z) - bwd(fr, 0, x, z, 0, fx),
            adj_at(7, x, z) - bwd(fr, 1, x, z, 1, fz),
            adj_at(8, x, z) - bwd(fr, 2, x, z, 2, fy),
            adj_at(9, x, z) - (fwd(fr, 0, x, z, 1, fx) + fwd(fr, 1, x, z, 0, fz)),
            adj_at(10, x, z) - (fwd(fr, 0, x, z, 2, fx) + fwd(fr, 2, x, z, 0, fy)),
            adj_at(11, x, z) - (fwd(fr, 1, x, z, 2, fz) + fwd(fr, 2, x, z, 1, fy)),
        ]
        p = adj_at(12, x, z) + (
            bwd(fr, 3, x, z, 0) + bwd(fr, 4, x, z, 1) + bwd(fr, 5, x, z, 2)
        )
        e = [strain[i, x, pl.ds(z, chunk), :] for i in range(7)]
        correlate(x, z, e[0:3], e[3:6], e[6], s, p, False)

    def velocity_back_1(x, z):
        v, q = velocity_bars(
            x, z, [adj_at(d, x, z) for d in range(3)], [adj_at(3 + d, x, z) for d in range(3)]
        )
        total = grad[3, x, pl.ds(z, chunk), :]
        for d in range(3):
            total = total + at(st, 3 + d, x, z) * (C3 * q[d] - C2 * v[d])
        grad[3, x, pl.ds(z, chunk), :] = -total

    over_cells(0, lambda x, z: velocities(x, z, st, 3, q1))
    over_cells(1, stresses)

    over_cells(2, lambda x, z: velocities(x, z, q1, 0, q2))
    over_cells(3, stress_back_2)
    over_cells(4, velocity_back_2)
    over_cells(5, stress_back_1)
    over_cells(6, velocity_back_1)

    if summed:
        low, high, rels = summed
        span = high - low
        keep, send = outs

        def split(x, carry):
            for k in range(4):
                at = pl.ds((k * span + x) * piece, piece)
                for i, rel in enumerate(rels):
                    keep[i, at, :] = grad[k, low + x, rows_of(rel), :]
                    send[i, at, :] = grad[k, low + x, rows_of(rel ^ 1), :]
            return carry

        lax.fori_loop(0, span, split, 0)


def march(me, fields, n, spans, gathered=(), pieces=(), summed=None, after=()):
    _, nx, nz, ny = fields[NAMES.index("adj")].shape
    outs = [pltpu.VMEM(f.shape, F32) for f in fields]
    if summed:
        part = (n // 2, 4 * (summed[1] - summed[0]) * (nz // n), ny)
        outs += [pltpu.VMEM(part, F32)] * 2
    lead = 1 + len(pieces) + len(after)
    work = sum(end - begin for begin, end in spans)
    result = pl.pallas_call(
        functools.partial(
            march_kernel, n=n, spans=spans, gathered=gathered, summed=summed, waits=len(after)
        ),
        out_shape=tuple(outs),
        in_specs=[SMEM] + [VMEM] * (len(pieces) + len(after) + len(fields)),
        out_specs=(VMEM,) * len(outs),
        input_output_aliases={lead + i: i for i in range(len(fields))},
        compiler_params=PARAMS,
        cost_estimate=cost(work * nz * ny, 100),
        name="march",
    )(me, *[in_vmem(x) for x in (*pieces, *after, *fields)])
    return result[: len(fields)], result[len(fields) :]


def join(a, b, after=()):
    def kernel(a_ref, b_ref, *refs):
        out = refs[-1]
        out[: a.shape[0]] = a_ref[...]
        out[a.shape[0] :] = b_ref[...]

    return pl.pallas_call(
        kernel,
        out_shape=pltpu.VMEM((a.shape[0] + b.shape[0], *a.shape[1:]), F32),
        in_specs=[VMEM] * (2 + len(after)),
        out_specs=VMEM,
        compiler_params=PARAMS,
        cost_estimate=cost(2 * a.size, 1),
        name="join",
    )(*[in_vmem(x) for x in (a, b, *after)])


def add_halves(keep, came):
    half = keep.shape[0] // 2

    def kernel(a, b, low, high):
        low[...] = a[:half] + b[:half]
        high[...] = a[half:] + b[half:]

    return pl.pallas_call(
        kernel,
        out_shape=(pltpu.VMEM((half, *keep.shape[1:]), F32),) * 2,
        in_specs=[VMEM] * 2,
        out_specs=(VMEM,) * 2,
        compiler_params=PARAMS,
        cost_estimate=cost(keep.size, 1),
        name="add_halves",
    )(in_vmem(keep), in_vmem(came))


def finish(terms, cuts, factor, shape, scale):
    _, nx, piece, ny = shape

    def kernel(*refs):
        factor_ref, out = refs[-2:]
        for part, (low, high) in enumerate(zip(cuts, cuts[1:])):
            for x in range(low, high):
                for k in range(4):
                    at = (k * (high - low) + x - low) * piece
                    at = slice(at, at + piece)
                    total = refs[2 * part][0, at, :] + refs[2 * part + 1][0, at, :]
                    out[k, x] = total * factor_ref[k, x] * scale

    flat = [in_vmem(t) for part in terms for t in part]
    return pl.pallas_call(
        kernel,
        out_shape=jax.ShapeDtypeStruct(shape, F32),
        in_specs=[VMEM] * (len(flat) + 1),
        out_specs=VMEM,
        compiler_params=PARAMS,
        name="finish",
    )(*flat, in_vmem(factor))


def partner(x, bit, n):
    return lax.ppermute(x, "shot", [(i, i ^ bit) for i in range(n)])


PASSES = 7


def per_device(
    forward_state,
    adjoint_state,
    source_amp,
    source_cell,
    receiver_cells,
    recorded,
    material,
    cell_class,
    class_factors,
):
    n = lax.axis_size("shot")
    me = lax.axis_index("shot").reshape(1)
    nx = material.shape[1]
    along_z = [b for b in (4, 8, 16, 32, 64, 128) if b < n]

    factor, *owns = own_model(me, class_factors, cell_class, material, 2)
    ways = ([*along_z[::-1], 2], [2, *along_z[::-1]])
    data, rels = list(owns), [[0], [0]]
    fields, token = None, ()
    for step in range(len(ways[0])):
        came = [partner(d, way[step], n) for d, way in zip(data, ways)]
        if step == len(ways[0]) - 1:
            fields = load_fields(
                source_cell,
                source_amp,
                receiver_cells,
                recorded,
                forward_state[0],
                adjoint_state[0],
                data,
            )
            token = (fields[NAMES.index("hits")],)
        data = [join(d, c, token) for d, c in zip(data, came)]
        rels = [[*r, *[i ^ way[step] for i in r]] for r, way in zip(rels, ways)]
    pieces = [p for d in data for p in (d, partner(d, 1, n))]
    gathered = [(0, nx // 2, rels[0]), (nx // 2, nx, rels[1])]

    back = [2, *along_z]
    rels = [0]
    for b in back[::-1]:
        rels = [*rels, *[i ^ b for i in rels]]
    cuts = [0, nx // 2, nx * 3 // 4, nx]
    done = [0] * PASSES
    terms, after = [], ()
    for low, high in zip(cuts, cuts[1:]):
        limits = [min(nx, high + PASSES - 1 - p) for p in range(PASSES)]
        spans = tuple((d, max(d, limit)) for d, limit in zip(done, limits))
        done = [end for _, end in spans]
        if after:
            half = PASSES // 2
            early = (*spans[:half], *[(begin, begin) for begin, _ in spans[half:]])
            spans = (*[(end, end) for _, end in spans[:half]], *spans[half:])
            fields, _ = march(me, fields, n, early)
        fields, (keep, send) = march(
            me, fields, n, spans, gathered, pieces, (low, high, rels), after
        )
        gathered, pieces = (), ()
        came = partner(send, 1, n)
        for b in back:
            keep, send = add_halves(keep, came)
            if b == back[0]:
                after = (keep,)
            came = partner(send, b, n)
        terms.append((keep, came))
    scale = 1.0 / float(forward_state.shape[0] * n) ** 0.5
    return finish(terms, cuts, factor, material.shape, scale)


def solution(mesh):
    placed = (
        P(("groups", "shot"), None, None, None, None),
        P(("groups", "shot"), None, None, None, None),
        P(("groups", "shot"), None),
        P(("groups", "shot")),
        P(("groups", "shot"), None),
        P(("groups", "shot"), None),
        P(None, "groups", "shot", None),
        P("groups", None, None),
        P(),
    )
    return jax.shard_map(
        per_device,
        mesh=mesh,
        in_specs=placed,
        out_specs=P(None, "groups", "shot", None),
        check_vma=False,
    )
```

profile of v0, /device:TPU:0, one launch (start us, length us, event | category | flops | bytes accessed | tf_op | source)
XLA Modules:
  0.0 71.0 jit_solution(8967262785862410943)
XLA Ops:
  0.0 1.1 %own_model.1 = (f32[4,16,4,128]{3,2,1,0:T(4,128)S(1)}, f32[1,128,128]{2,1,0:T(8,128)S(1)}, f32[1,128,128]{2,1,0:T(8,128)S(1)}) custom-call(s32[1]{0:T(128)} %bitcast.me_ref, f32[4,4]{1,0:T(4,128)} %class_factors.1, s32[16,64,128]{2,1,0:T(8,128)} %classes_hbm.1, f32[4,16,4,128]{3,2,1,0:T(4,128)} %material_hbm.1), custom_call_target="tpu_custom_call" | custom-call | flops 327680 | bytes 131072 | tf_op jit(solution)/shard_map/own_model/pallas_call | solution.py:87
  1.2 4.1 %collective-permute-start = (f32[1,128,128]{2,1,0:T(8,128)S(1)}, f32[1,128,128]{2,1,0:T(8,128)S(1)}, u32[]{:S(2)}, u32[]{:S(2)}) collective-permute-start(f32[1,128,128]{2,1,0:T(8,128)S(1)} %get-tuple-element.92.a_ref), channel_id=1, source_target_pairs={{0,8},{1,9},{2,10},{3,11},{4,12},{5,13},{6,14},{7,15},{8,0},{9,1},... | collective-permute-start | bytes 196616 | tf_op jit(solution)/shard_map/ppermute | solution.py:524
  5.3 1.5 %collective-permute-start.3 = (f32[1,128,128]{2,1,0:T(8,128)S(1)}, f32[1,128,128]{2,1,0:T(8,128)S(1)}, u32[]{:S(2)}, u32[]{:S(2)}) collective-permute-start(f32[1,128,128]{2,1,0:T(8,128)S(1)} %get-tuple-element.93.a_ref), channel_id=1, source_target_pairs={{0,2},{1,3},{2,0},{3,1},{4,6},{5,7},{6,4},{7,5},{8,10},{9,11},{10,... | collective-permute-start | bytes 196616 | tf_op jit(solution)/shard_map/ppermute | solution.py:524
  6.8 2.1 %collective-permute-done.b_ref = f32[1,128,128]{2,1,0:T(8,128)S(1)} collective-permute-done((f32[1,128,128]{2,1,0:T(8,128)S(1)}, f32[1,128,128]{2,1,0:T(8,128)S(1)}, u32[]{:S(2)}, u32[]{:S(2)}) %collective-permute-start) | collective-permute-done | bytes 65568 | tf_op jit(solution)/shard_map/ppermute | solution.py:524
  8.9 0.6 collective-permute-start.1
  9.5 0.0 collective-permute-done.3.b_ref
  9.6 3.4 %collective-permute-start.4 = (f32[2,128,128]{2,1,0:T(8,128)S(1)}, f32[2,128,128]{2,1,0:T(8,128)S(1)}, u32[]{:S(2)}, u32[]{:S(2)}) collective-permute-start(f32[2,128,128]{2,1,0:T(8,128)S(1)} %join.8.a_ref), channel_id=1, source_target_pairs={{0,8},{1,9},{2,10},{3,11},{4,12},{5,13},{6,14},{7,15},{8,0},{9,1},... | collective-permute-start | bytes 393224 | tf_op jit(solution)/shard_map/ppermute | solution.py:524
  13.0 3.0 %collective-permute-done.1.b_ref = f32[2,128,128]{2,1,0:T(8,128)S(1)} collective-permute-done((f32[2,128,128]{2,1,0:T(8,128)S(1)}, f32[2,128,128]{2,1,0:T(8,128)S(1)}, u32[]{:S(2)}, u32[]{:S(2)}) %collective-permute-start.1) | collective-permute-done | bytes 131104 | tf_op jit(solution)/shard_map/ppermute | solution.py:524
  16.0 2.0 %collective-permute-start.2 = (f32[4,128,128]{2,1,0:T(8,128)S(1)}, f32[4,128,128]{2,1,0:T(8,128)S(1)}, u32[]{:S(2)}, u32[]{:S(2)}) collective-permute-start(f32[4,128,128]{2,1,0:T(8,128)S(1)} %join.7.refs_0_.a_ref), channel_id=1, source_target_pairs={{0,2},{1,3},{2,0},{3,1},{4,6},{5,7},{6,4},{7,5},{8,10},{9,11},{10,... | collective-permute-start | bytes 786440 | tf_op jit(solution)/shard_map/ppermute | solution.py:524
  18.0 0.9 %collective-permute-done.4.b_ref = f32[2,128,128]{2,1,0:T(8,128)S(1)} collective-permute-done((f32[2,128,128]{2,1,0:T(8,128)S(1)}, f32[2,128,128]{2,1,0:T(8,128)S(1)}, u32[]{:S(2)}, u32[]{:S(2)}) %collective-permute-start.4) | collective-permute-done | bytes 131104 | tf_op jit(solution)/shard_map/ppermute | solution.py:524
  18.9 0.3 collective-permute-start.6
  19.9 5.4 %load_fields.1 = (f32[13,18,80,128]{3,2,1,0:T(8,128)S(1)}, f32[3,18,80,128]{3,2,1,0:T(8,128)S(1)}, f32[3,18,80,128]{3,2,1,0:T(8,128)S(1)}, f32[7,18,80,128]{3,2,...) custom-call(s32[1]{0:T(128)S(6)} %copy.130.src_cell, ...), custom_call_target="tpu_custom_call" | custom-call | flops 19660800 | bytes 524288 | tf_op jit(solution)/shard_map/load_fields/pallas_call | solution.py:195
  25.3 0.0 collective-permute-done.2.b_ref
  25.4 0.1 collective-permute-start.5
  25.5 0.0 collective-permute-done.6.b_ref
  25.5 0.5 collective-permute-start.7
  26.1 1.3 %collective-permute-done.5.refs_1_ = f32[8,128,128]{2,1,0:T(8,128)S(1)} collective-permute-done((f32[8,128,128]{2,1,0:T(8,128)S(1)}, f32[8,128,128]{2,1,0:T(8,128)S(1)}, u32[]{:S(2)}, u32[]{:S(2)}) %collective-permute-start.5) | collective-permute-done | bytes 524320 | tf_op jit(solution)/shard_map/ppermute | solution.py:524
  27.4 0.7 %collective-permute-done.7.refs_3_ = f32[8,128,128]{2,1,0:T(8,128)S(1)} collective-permute-done((f32[8,128,128]{2,1,0:T(8,128)S(1)}, f32[8,128,128]{2,1,0:T(8,128)S(1)}, u32[]{:S(2)}, u32[]{:S(2)}) %collective-permute-start.7) | collective-permute-done | bytes 524320 | tf_op jit(solution)/shard_map/ppermute | solution.py:524
  28.1 10.5 %march.5 = (f32[13,18,80,128]{3,2,1,0:T(8,128)S(1)}, f32[3,18,80,128]{3,2,1,0:T(8,128)S(1)}, f32[3,18,80,128]{3,2,1,0:T(8,128)S(1)}, f32[7,18,80,128]{3,2,1,0:T(...) custom-call(s32[1]{0:T(128)} %bitcast.me_ref, ...), custom_call_target="tpu_custom_call", output_to_operand_aliasing={{0}: (5, {}), {1}: (6, {}), {2}: (7, {}), {3}: (8, {}), {4}... | custom-call | flops 63078400 | bytes 2523136 | tf_op jit(solution)/shard_map/march/pallas_call | solution.py:449
  38.6 0.2 collective-permute-start.8
  38.9 1.1 %march.6 = (f32[13,18,80,128]{3,2,1,0:T(8,128)S(1)}, f32[3,18,80,128]{3,2,1,0:T(8,128)S(1)}, f32[3,18,80,128]{3,2,1,0:T(8,128)S(1)}, f32[7,18,80,128]{3,2,1,0:T(...) custom-call(s32[1]{0:T(128)} %bitcast.me_ref, ...), custom_call_target="tpu_custom_call", output_to_operand_aliasing={{0}: (1, {}), {1}: (2, {}), {2}: (3, {}), {3}: (4, {}), {4}... | custom-call | flops 7372800 | bytes 294912 | tf_op jit(solution)/shard_map/march/pallas_call | solution.py:449
  39.9 0.7 collective-permute-done.8.b
  40.6 0.1 add_halves.9
  40.7 2.2 %march.7 = (f32[13,18,80,128]{3,2,1,0:T(8,128)S(1)}, f32[3,18,80,128]{3,2,1,0:T(8,128)S(1)}, f32[3,18,80,128]{3,2,1,0:T(8,128)S(1)}, f32[7,18,80,128]{3,2,1,0:T(...) custom-call(s32[1]{0:T(128)} %bitcast.me_ref, ...), custom_call_target="tpu_custom_call", output_to_operand_aliasing={{0}: (2, {}), {1}: (3, {}), {2}: (4, {}), {3}: (5, {}), {4}... | custom-call | flops 13107200 | bytes 524288 | tf_op jit(solution)/shard_map/march/pallas_call | solution.py:449
  42.9 0.2 collective-permute-start.12
  43.1 1.4 %collective-permute-done.12.b = f32[8,64,128]{2,1,0:T(8,128)S(1)} collective-permute-done((f32[8,64,128]{2,1,0:T(8,128)S(1)}, f32[8,64,128]{2,1,0:T(8,128)S(1)}, u32[]{:S(2)}, u32[]{:S(2)}) %collective-permute-start.12) | collective-permute-done | bytes 262176 | tf_op jit(solution)/shard_map/ppermute | solution.py:524
  44.5 1.4 %march.9 = (f32[13,18,80,128]{3,2,1,0:T(8,128)S(1)}, f32[3,18,80,128]{3,2,1,0:T(8,128)S(1)}, f32[3,18,80,128]{3,2,1,0:T(8,128)S(1)}, f32[7,18,80,128]{3,2,1,0:T(...) custom-call(s32[1]{0:T(128)} %bitcast.me_ref, ...), custom_call_target="tpu_custom_call", output_to_operand_aliasing={{0}: (2, {}), {1}: (3, {}), {2}: (4, {}), {3}: (5, {}), {4}... | custom-call | flops 8192000 | bytes 327680 | tf_op jit(solution)/shard_map/march/pallas_call | solution.py:449
  45.9 0.2 collective-permute-start.16
  46.1 1.5 %collective-permute-start.9 = (f32[4,128,128]{2,1,0:T(8,128)S(1)}, f32[4,128,128]{2,1,0:T(8,128)S(1)}, u32[]{:S(2)}, u32[]{:S(2)}) collective-permute-start(f32[4,128,128]{2,1,0:T(8,128)S(1)} %get-tuple-element.109), channel_id=1, source_target_pairs={{0,2},{1,3},{2,0},{3,1},{4,6},{5,7},{6,4},{7,5},{8,10},{9,11},{10,... | collective-permute-start | bytes 786440 | tf_op jit(solution)/shard_map/ppermute | solution.py:524
  47.7 0.5 collective-permute-start.13
  48.2 0.0 collective-permute-done.16.b
  48.2 1.6 %collective-permute-start.17 = (f32[4,64,128]{2,1,0:T(8,128)S(1)}, f32[4,64,128]{2,1,0:T(8,128)S(1)}, u32[]{:S(2)}, u32[]{:S(2)}) collective-permute-start(f32[4,64,128]{2,1,0:T(8,128)S(1)} %get-tuple-element.173), channel_id=1, source_target_pairs={{0,2},{1,3},{2,0},{3,1},{4,6},{5,7},{6,4},{7,5},{8,10},{9,11},{10,... | collective-permute-start | bytes 393224 | tf_op jit(solution)/shard_map/ppermute | solution.py:524
  49.8 5.5 %collective-permute-done.9.b = f32[4,128,128]{2,1,0:T(8,128)S(1)} collective-permute-done((f32[4,128,128]{2,1,0:T(8,128)S(1)}, f32[4,128,128]{2,1,0:T(8,128)S(1)}, u32[]{:S(2)}, u32[]{:S(2)}) %collective-permute-start.9) | collective-permute-done | bytes 262176 | tf_op jit(solution)/shard_map/ppermute | solution.py:524
  55.3 1.9 %collective-permute-start.10 = (f32[2,128,128]{2,1,0:T(8,128)S(1)}, f32[2,128,128]{2,1,0:T(8,128)S(1)}, u32[]{:S(2)}, u32[]{:S(2)}) collective-permute-start(f32[2,128,128]{2,1,0:T(8,128)S(1)} %get-tuple-element.111), channel_id=1, source_target_pairs={{0,4},{1,5},{2,6},{3,7},{4,0},{5,1},{6,2},{7,3},{8,12},{9,13},{10,... | collective-permute-start | bytes 393224 | tf_op jit(solution)/shard_map/ppermute | solution.py:524
  57.2 0.9 %collective-permute-done.13.b = f32[4,64,128]{2,1,0:T(8,128)S(1)} collective-permute-done((f32[4,64,128]{2,1,0:T(8,128)S(1)}, f32[4,64,128]{2,1,0:T(8,128)S(1)}, u32[]{:S(2)}, u32[]{:S(2)}) %collective-permute-start.13) | collective-permute-done | bytes 131104 | tf_op jit(solution)/shard_map/ppermute | solution.py:524
  58.1 1.9 %collective-permute-start.14 = (f32[2,64,128]{2,1,0:T(8,128)S(1)}, f32[2,64,128]{2,1,0:T(8,128)S(1)}, u32[]{:S(2)}, u32[]{:S(2)}) collective-permute-start(f32[2,64,128]{2,1,0:T(8,128)S(1)} %get-tuple-element.143), channel_id=1, source_target_pairs={{0,4},{1,5},{2,6},{3,7},{4,0},{5,1},{6,2},{7,3},{8,12},{9,13},{10,... | collective-permute-start | bytes 196616 | tf_op jit(solution)/shard_map/ppermute | solution.py:524
  60.0 0.4 collective-permute-done.17.b
  60.4 1.9 %collective-permute-start.18 = (f32[2,64,128]{2,1,0:T(8,128)S(1)}, f32[2,64,128]{2,1,0:T(8,128)S(1)}, u32[]{:S(2)}, u32[]{:S(2)}) collective-permute-start(f32[2,64,128]{2,1,0:T(8,128)S(1)} %get-tuple-element.175), channel_id=1, source_target_pairs={{0,4},{1,5},{2,6},{3,7},{4,0},{5,1},{6,2},{7,3},{8,12},{9,13},{10,... | collective-permute-start | bytes 196616 | tf_op jit(solution)/shard_map/ppermute | solution.py:524
  62.2 0.0 collective-permute-done.10.b
  62.2 1.5 %collective-permute-start.11 = (f32[1,128,128]{2,1,0:T(8,128)S(1)}, f32[1,128,128]{2,1,0:T(8,128)S(1)}, u32[]{:S(2)}, u32[]{:S(2)}) collective-permute-start(f32[1,128,128]{2,1,0:T(8,128)S(1)} %get-tuple-element.113), channel_id=1, source_target_pairs={{0,8},{1,9},{2,10},{3,11},{4,12},{5,13},{6,14},{7,15},{8,0},{9,1},... | collective-permute-start | bytes 196616 | tf_op jit(solution)/shard_map/ppermute | solution.py:524
  63.7 0.0 collective-permute-done.14.b
  63.8 1.6 %collective-permute-start.15 = (f32[1,64,128]{2,1,0:T(8,128)S(1)}, f32[1,64,128]{2,1,0:T(8,128)S(1)}, u32[]{:S(2)}, u32[]{:S(2)}) collective-permute-start(f32[1,64,128]{2,1,0:T(8,128)S(1)} %get-tuple-element.145), channel_id=1, source_target_pairs={{0,8},{1,9},{2,10},{3,11},{4,12},{5,13},{6,14},{7,15},{8,0},{9,1},... | collective-permute-start | bytes 98312 | tf_op jit(solution)/shard_map/ppermute | solution.py:524
  65.3 0.0 collective-permute-done.18.b
  65.3 2.2 %collective-permute-start.19 = (f32[1,64,128]{2,1,0:T(8,128)S(1)}, f32[1,64,128]{2,1,0:T(8,128)S(1)}, u32[]{:S(2)}, u32[]{:S(2)}) collective-permute-start(f32[1,64,128]{2,1,0:T(8,128)S(1)} %get-tuple-element.177), channel_id=1, source_target_pairs={{0,8},{1,9},{2,10},{3,11},{4,12},{5,13},{6,14},{7,15},{8,0},{9,1},... | collective-permute-start | bytes 98312 | tf_op jit(solution)/shard_map/ppermute | solution.py:524
  67.5 1.8 %collective-permute-done.11.refs_1_ = f32[1,128,128]{2,1,0:T(8,128)S(1)} collective-permute-done((f32[1,128,128]{2,1,0:T(8,128)S(1)}, f32[1,128,128]{2,1,0:T(8,128)S(1)}, u32[]{:S(2)}, u32[]{:S(2)}) %collective-permute-start.11) | collective-permute-done | bytes 65568 | tf_op jit(solution)/shard_map/ppermute | solution.py:524
  69.3 0.7 collective-permute-done.15.refs_3_
  70.0 0.4 collective-permute-done.19.refs_5_
  70.3 0.7 %finish.1 = f32[4,16,4,128]{3,2,1,0:T(4,128)} custom-call(f32[1,128,128]{2,1,0:T(8,128)S(1)} %get-tuple-element.112.refs_0_, f32[1,128,128]{2,1,0:T(8,128)S(1)} %collective-permute-done.11.refs_1_, f32[1,64,128]{2,1,0:T(8,128)S(1)} %get-tuple-element.144.refs_2_, f32[1,64,128]{2,1,0:T(8,128)S(1)} %collective-permute-done.15.refs_3_, ...), custom_call_target="tpu_custom_call" | custom-call | tf_op jit(solution)/shard_map/finish/pallas_call | solution.py:513
  (15 shorter events, 0.3 us)
Async XLA Ops:
  1.2 7.8 %collective-permute-start = (f32[1,128,128]{2,1,0:T(8,128)S(1)}, f32[1,128,128]{2,1,0:T(8,128)S(1)}, u32[]{:S(2)}, u32[]{:S(2)}) collective-permute-start(f32[1,128,128]{2,1,0:T(8,128)S(1)} %get-tuple-element.92.a_ref), channel_id=1, source_target_pairs={{0,8},{1,9},{2,10},{3,11},{4,12},{5,13},{6,14},{7,15},{8,0},{9,1},... | collective-permute-start | bytes 196616 | tf_op jit(solution)/shard_map/ppermute | solution.py:524
  5.3 4.3 %collective-permute-start.3 = (f32[1,128,128]{2,1,0:T(8,128)S(1)}, f32[1,128,128]{2,1,0:T(8,128)S(1)}, u32[]{:S(2)}, u32[]{:S(2)}) collective-permute-start(f32[1,128,128]{2,1,0:T(8,128)S(1)} %get-tuple-element.93.a_ref), channel_id=1, source_target_pairs={{0,2},{1,3},{2,0},{3,1},{4,6},{5,7},{6,4},{7,5},{8,10},{9,11},{10,... | collective-permute-start | bytes 196616 | tf_op jit(solution)/shard_map/ppermute | solution.py:524
  8.9 7.1 %collective-permute-start.1 = (f32[2,128,128]{2,1,0:T(8,128)S(1)}, f32[2,128,128]{2,1,0:T(8,128)S(1)}, u32[]{:S(2)}, u32[]{:S(2)}) collective-permute-start(f32[2,128,128]{2,1,0:T(8,128)S(1)} %join.6.a_ref), channel_id=1, source_target_pairs={{0,4},{1,5},{2,6},{3,7},{4,0},{5,1},{6,2},{7,3},{8,12},{9,13},{10,... | collective-permute-start | bytes 393224 | tf_op jit(solution)/shard_map/ppermute | solution.py:524
  9.6 9.3 %collective-permute-start.4 = (f32[2,128,128]{2,1,0:T(8,128)S(1)}, f32[2,128,128]{2,1,0:T(8,128)S(1)}, u32[]{:S(2)}, u32[]{:S(2)}) collective-permute-start(f32[2,128,128]{2,1,0:T(8,128)S(1)} %join.8.a_ref), channel_id=1, source_target_pairs={{0,8},{1,9},{2,10},{3,11},{4,12},{5,13},{6,14},{7,15},{8,0},{9,1},... | collective-permute-start | bytes 393224 | tf_op jit(solution)/shard_map/ppermute | solution.py:524
  16.0 9.3 %collective-permute-start.2 = (f32[4,128,128]{2,1,0:T(8,128)S(1)}, f32[4,128,128]{2,1,0:T(8,128)S(1)}, u32[]{:S(2)}, u32[]{:S(2)}) collective-permute-start(f32[4,128,128]{2,1,0:T(8,128)S(1)} %join.7.refs_0_.a_ref), channel_id=1, source_target_pairs={{0,2},{1,3},{2,0},{3,1},{4,6},{5,7},{6,4},{7,5},{8,10},{9,11},{10,... | collective-permute-start | bytes 786440 | tf_op jit(solution)/shard_map/ppermute | solution.py:524
  18.9 6.5 %collective-permute-start.6 = (f32[4,128,128]{2,1,0:T(8,128)S(1)}, f32[4,128,128]{2,1,0:T(8,128)S(1)}, u32[]{:S(2)}, u32[]{:S(2)}) collective-permute-start(f32[4,128,128]{2,1,0:T(8,128)S(1)} %join.9.refs_1_.a_ref), channel_id=1, source_target_pairs={{0,4},{1,5},{2,6},{3,7},{4,0},{5,1},{6,2},{7,3},{8,12},{9,13},{10,... | collective-permute-start | bytes 786440 | tf_op jit(solution)/shard_map/ppermute | solution.py:524
  25.4 2.0 %collective-permute-start.5 = (f32[8,128,128]{2,1,0:T(8,128)S(1)}, f32[8,128,128]{2,1,0:T(8,128)S(1)}, u32[]{:S(2)}, u32[]{:S(2)}) collective-permute-start(f32[8,128,128]{2,1,0:T(8,128)S(1)} %join.10.refs_0_), channel_id=1, source_target_pairs={{0,1},{1,0},{2,3},{3,2},{4,5},{5,4},{6,7},{7,6},{8,9},{9,8},{10,11... | collective-permute-start | bytes 1572872 | tf_op jit(solution)/shard_map/ppermute | solution.py:524
  25.5 2.6 %collective-permute-start.7 = (f32[8,128,128]{2,1,0:T(8,128)S(1)}, f32[8,128,128]{2,1,0:T(8,128)S(1)}, u32[]{:S(2)}, u32[]{:S(2)}) collective-permute-start(f32[8,128,128]{2,1,0:T(8,128)S(1)} %join.11.refs_2_), channel_id=1, source_target_pairs={{0,1},{1,0},{2,3},{3,2},{4,5},{5,4},{6,7},{7,6},{8,9},{9,8},{10,11... | collective-permute-start | bytes 1572872 | tf_op jit(solution)/shard_map/ppermute | solution.py:524
  38.6 2.0 %collective-permute-start.8 = (f32[8,128,128]{2,1,0:T(8,128)S(1)}, f32[8,128,128]{2,1,0:T(8,128)S(1)}, u32[]{:S(2)}, u32[]{:S(2)}) collective-permute-start(f32[8,128,128]{2,1,0:T(8,128)S(1)} %get-tuple-element.107), channel_id=1, source_target_pairs={{0,1},{1,0},{2,3},{3,2},{4,5},{5,4},{6,7},{7,6},{8,9},{9,8},{10,11... | collective-permute-start | bytes 1572872 | tf_op jit(solution)/shard_map/ppermute | solution.py:524
  42.9 1.6 %collective-permute-start.12 = (f32[8,64,128]{2,1,0:T(8,128)S(1)}, f32[8,64,128]{2,1,0:T(8,128)S(1)}, u32[]{:S(2)}, u32[]{:S(2)}) collective-permute-start(f32[8,64,128]{2,1,0:T(8,128)S(1)} %get-tuple-element.139), channel_id=1, source_target_pairs={{0,1},{1,0},{2,3},{3,2},{4,5},{5,4},{6,7},{7,6},{8,9},{9,8},{10,11... | collective-permute-start | bytes 786440 | tf_op jit(solution)/shard_map/ppermute | solution.py:524
  45.9 2.2 %collective-permute-start.16 = (f32[8,64,128]{2,1,0:T(8,128)S(1)}, f32[8,64,128]{2,1,0:T(8,128)S(1)}, u32[]{:S(2)}, u32[]{:S(2)}) collective-permute-start(f32[8,64,128]{2,1,0:T(8,128)S(1)} %get-tuple-element.171), channel_id=1, source_target_pairs={{0,1},{1,0},{2,3},{3,2},{4,5},{5,4},{6,7},{7,6},{8,9},{9,8},{10,11... | collective-permute-start | bytes 786440 | tf_op jit(solution)/shard_map/ppermute | solution.py:524
  46.1 9.1 %collective-permute-start.9 = (f32[4,128,128]{2,1,0:T(8,128)S(1)}, f32[4,128,128]{2,1,0:T(8,128)S(1)}, u32[]{:S(2)}, u32[]{:S(2)}) collective-permute-start(f32[4,128,128]{2,1,0:T(8,128)S(1)} %get-tuple-element.109), channel_id=1, source_target_pairs={{0,2},{1,3},{2,0},{3,1},{4,6},{5,7},{6,4},{7,5},{8,10},{9,11},{10,... | collective-permute-start | bytes 786440 | tf_op jit(solution)/shard_map/ppermute | solution.py:524
  47.7 10.4 %collective-permute-start.13 = (f32[4,64,128]{2,1,0:T(8,128)S(1)}, f32[4,64,128]{2,1,0:T(8,128)S(1)}, u32[]{:S(2)}, u32[]{:S(2)}) collective-permute-start(f32[4,64,128]{2,1,0:T(8,128)S(1)} %get-tuple-element.141), channel_id=1, source_target_pairs={{0,2},{1,3},{2,0},{3,1},{4,6},{5,7},{6,4},{7,5},{8,10},{9,11},{10,... | collective-permute-start | bytes 393224 | tf_op jit(solution)/shard_map/ppermute | solution.py:524
  48.2 12.1 %collective-permute-start.17 = (f32[4,64,128]{2,1,0:T(8,128)S(1)}, f32[4,64,128]{2,1,0:T(8,128)S(1)}, u32[]{:S(2)}, u32[]{:S(2)}) collective-permute-start(f32[4,64,128]{2,1,0:T(8,128)S(1)} %get-tuple-element.173), channel_id=1, source_target_pairs={{0,2},{1,3},{2,0},{3,1},{4,6},{5,7},{6,4},{7,5},{8,10},{9,11},{10,... | collective-permute-start | bytes 393224 | tf_op jit(solution)/shard_map/ppermute | solution.py:524
  55.3 6.9 %collective-permute-start.10 = (f32[2,128,128]{2,1,0:T(8,128)S(1)}, f32[2,128,128]{2,1,0:T(8,128)S(1)}, u32[]{:S(2)}, u32[]{:S(2)}) collective-permute-start(f32[2,128,128]{2,1,0:T(8,128)S(1)} %get-tuple-element.111), channel_id=1, source_target_pairs={{0,4},{1,5},{2,6},{3,7},{4,0},{5,1},{6,2},{7,3},{8,12},{9,13},{10,... | collective-permute-start | bytes 393224 | tf_op jit(solution)/shard_map/ppermute | solution.py:524
  58.1 5.6 %collective-permute-start.14 = (f32[2,64,128]{2,1,0:T(8,128)S(1)}, f32[2,64,128]{2,1,0:T(8,128)S(1)}, u32[]{:S(2)}, u32[]{:S(2)}) collective-permute-start(f32[2,64,128]{2,1,0:T(8,128)S(1)} %get-tuple-element.143), channel_id=1, source_target_pairs={{0,4},{1,5},{2,6},{3,7},{4,0},{5,1},{6,2},{7,3},{8,12},{9,13},{10,... | collective-permute-start | bytes 196616 | tf_op jit(solution)/shard_map/ppermute | solution.py:524
  60.4 4.9 %collective-permute-start.18 = (f32[2,64,128]{2,1,0:T(8,128)S(1)}, f32[2,64,128]{2,1,0:T(8,128)S(1)}, u32[]{:S(2)}, u32[]{:S(2)}) collective-permute-start(f32[2,64,128]{2,1,0:T(8,128)S(1)} %get-tuple-element.175), channel_id=1, source_target_pairs={{0,4},{1,5},{2,6},{3,7},{4,0},{5,1},{6,2},{7,3},{8,12},{9,13},{10,... | collective-permute-start | bytes 196616 | tf_op jit(solution)/shard_map/ppermute | solution.py:524
  62.2 7.1 %collective-permute-start.11 = (f32[1,128,128]{2,1,0:T(8,128)S(1)}, f32[1,128,128]{2,1,0:T(8,128)S(1)}, u32[]{:S(2)}, u32[]{:S(2)}) collective-permute-start(f32[1,128,128]{2,1,0:T(8,128)S(1)} %get-tuple-element.113), channel_id=1, source_target_pairs={{0,8},{1,9},{2,10},{3,11},{4,12},{5,13},{6,14},{7,15},{8,0},{9,1},... | collective-permute-start | bytes 196616 | tf_op jit(solution)/shard_map/ppermute | solution.py:524
  63.8 6.2 %collective-permute-start.15 = (f32[1,64,128]{2,1,0:T(8,128)S(1)}, f32[1,64,128]{2,1,0:T(8,128)S(1)}, u32[]{:S(2)}, u32[]{:S(2)}) collective-permute-start(f32[1,64,128]{2,1,0:T(8,128)S(1)} %get-tuple-element.145), channel_id=1, source_target_pairs={{0,8},{1,9},{2,10},{3,11},{4,12},{5,13},{6,14},{7,15},{8,0},{9,1},... | collective-permute-start | bytes 98312 | tf_op jit(solution)/shard_map/ppermute | solution.py:524
  65.3 5.0 %collective-permute-start.19 = (f32[1,64,128]{2,1,0:T(8,128)S(1)}, f32[1,64,128]{2,1,0:T(8,128)S(1)}, u32[]{:S(2)}, u32[]{:S(2)}) collective-permute-start(f32[1,64,128]{2,1,0:T(8,128)S(1)} %get-tuple-element.177), channel_id=1, source_target_pairs={{0,8},{1,9},{2,10},{3,11},{4,12},{5,13},{6,14},{7,15},{8,0},{9,1},... | collective-permute-start | bytes 98312 | tf_op jit(solution)/shard_map/ppermute | solution.py:524
where the time goes:
time: 71.2 us; the launch traced here: 71 us
  starting transfers between devices  27.6 us (39%)
  Pallas kernels  22.8 us (32%)
  waiting for transfers between devices  19.8 us (28%)
  between operations  0.81 us (1%)
    ppermute x20, starting transfers between devices, partner(): return lax.ppermute(x, 'shot', [(i, i ^ bit) for i in range(n)])  27.6 us
    ppermute x20, waiting for transfers between devices, partner(): return lax.ppermute(x, 'shot', [(i, i ^ bit) for i in range(n)])  19.8 us
    pallas_call x5, Pallas kernels, march(): pl.pallas_call(functools.partial(march_kernel, n=n, spans=spans, gathered...  15.2 us
    pallas_call x1, Pallas kernels, load_fields(): pl.pallas_call(functools.partial(load_kernel, waits=len(after)), out_shap...  5.42 us
  transfers between devices with their start and end apart: 20, of which 13 were waited for; matrix products, arithmetic and copies ran while one was open for 0% of the time, Pallas kernels for 10%

commit v1 on v0

--- a/solution.py
+++ b/solution.py
@@ -19,6 +19,7 @@
 
 GUARD = 8
 CHUNK = 16
+UNROLL = 8
 F32 = jnp.float32
 BF16 = jnp.bfloat16
 PARAMS = pltpu.CompilerParams(vmem_limit_bytes=12 * 1024 * 1024)
@@ -278,13 +279,20 @@
     def over_cells(number, body):
         begin, end = spans[number]
 
-        def plane(x, carry):
+        def plane(x):
             for z in range(0, nz, chunk):
                 body(x, z)
+
+        def planes(i, carry):
+            for x in range(UNROLL):
+                plane(begin + i * UNROLL + x)
             return carry
 
-        if end > begin:
-            lax.fori_loop(begin, end, plane, 0)
+        whole = (end - begin) // UNROLL
+        if whole:
+            lax.fori_loop(0, whole, planes, 0)
+        for x in range(begin + whole * UNROLL, end):
+            plane(x)
 
     def mod(k, x, z):
         return model[k, x, pl.ds(z, chunk), :]
@@ -478,22 +486,23 @@
     )(*[in_vmem(x) for x in (a, b, *after)])
 
 
-def add_halves(keep, came):
+def add_halves(keep, came, after=()):
     half = keep.shape[0] // 2
 
-    def kernel(a, b, low, high):
+    def kernel(a, b, *refs):
+        low, high = refs[-2:]
         low[...] = a[:half] + b[:half]
         high[...] = a[half:] + b[half:]
 
     return pl.pallas_call(
         kernel,
         out_shape=(pltpu.VMEM((half, *keep.shape[1:]), F32),) * 2,
-        in_specs=[VMEM] * 2,
+        in_specs=[VMEM] * (2 + len(after)),
         out_specs=(VMEM,) * 2,
         compiler_params=PARAMS,
         cost_estimate=cost(keep.size, 1),
         name="add_halves",
-    )(in_vmem(keep), in_vmem(came))
+    )(*[in_vmem(x) for x in (keep, came, *after)])
 
 
 def finish(terms, cuts, factor, shape, scale):
@@ -565,31 +574,22 @@
     pieces = [p for d in data for p in (d, partner(d, 1, n))]
     gathered = [(0, nx // 2, rels[0]), (nx // 2, nx, rels[1])]
 
-    back = [2, *along_z]
-    rels = [0]
-    for b in back[::-1]:
-        rels = [*rels, *[i ^ b for i in rels]]
-    cuts = [0, nx // 2, nx * 3 // 4, nx]
+    backs = ([2, *along_z], [*along_z, 2])
+    cuts = [0, nx * 5 // 8, nx]
     done = [0] * PASSES
-    terms, after = [], ()
-    for low, high in zip(cuts, cuts[1:]):
+    terms = []
+    for low, high, back in zip(cuts, cuts[1:], backs):
+        rels = [0]
+        for b in back[::-1]:
+            rels = [*rels, *[i ^ b for i in rels]]
         limits = [min(nx, high + PASSES - 1 - p) for p in range(PASSES)]
         spans = tuple((d, max(d, limit)) for d, limit in zip(done, limits))
         done = [end for _, end in spans]
-        if after:
-            half = PASSES // 2
-            early = (*spans[:half], *[(begin, begin) for begin, _ in spans[half:]])
-            spans = (*[(end, end) for _, end in spans[:half]], *spans[half:])
-            fields, _ = march(me, fields, n, early)
-        fields, (keep, send) = march(
-            me, fields, n, spans, gathered, pieces, (low, high, rels), after
-        )
+        fields, (keep, send) = march(me, fields, n, spans, gathered, pieces, (low, high, rels))
         gathered, pieces = (), ()
         came = partner(send, 1, n)
         for b in back:
             keep, send = add_halves(keep, came)
-            if b == back[0]:
-                after = (keep,)
             came = partner(send, b, n)
         terms.append((keep, came))
     scale = 1.0 / float(forward_state.shape[0] * n) ** 0.5

time: 71.2 us -> 63.3 us (0.89)
  Pallas kernels: 22.8 us -> 17.8 us
  starting transfers between devices: 27.6 us -> 23.9 us
  waiting for transfers between devices: 19.8 us -> 20.7 us
    pallas_call x5 -> x2, Pallas kernels: 15.2 us -> 10.2 us  [march(): pl.pallas_call(functools.partial(march_kernel, n=n, spans=spans, gathered...]
    ppermute x20 -> x16, starting transfers between devices: 27.6 us -> 23.9 us  [partner(): return lax.ppermute(x, 'shot', [(i, i ^ bit) for i in range(n)])]
    ppermute x20 -> x16, waiting for transfers between devices: 19.8 us -> 20.7 us  [partner(): return lax.ppermute(x, 'shot', [(i, i ^ bit) for i in range(n)])]
  transfers between devices with their start and end apart: 20 -> 16, of which waited for: 13 -> 8; matrix products, arithmetic and copies ran while one was open for 0% -> 0% of each run, Pallas kernels for 10% -> 12%
where the time goes in v1:
time: 63.3 us; the launch traced here: 63.1 us
  starting transfers between devices  23.9 us (38%)
  waiting for transfers between devices  20.7 us (33%)
  Pallas kernels  17.8 us (28%)
  between operations  0.78 us (1%)
    ppermute x16, starting transfers between devices, partner(): return lax.ppermute(x, 'shot', [(i, i ^ bit) for i in range(n)])  23.9 us
    ppermute x16, waiting for transfers between devices, partner(): return lax.ppermute(x, 'shot', [(i, i ^ bit) for i in range(n)])  20.7 us
    pallas_call x2, Pallas kernels, march(): pl.pallas_call(functools.partial(march_kernel, n=n, spans=spans, gathered...  10.2 us
    pallas_call x1, Pallas kernels, load_fields(): pl.pallas_call(functools.partial(load_kernel, waits=len(after)), out_shap...  5.42 us
  transfers between devices with their start and end apart: 16, of which 8 were waited for; matrix products, arithmetic and copies ran while one was open for 0% of the time, Pallas kernels for 12%

profile of v1, /device:TPU:0, one launch (start us, length us, event | category | flops | bytes accessed | tf_op | source)
XLA Modules:
  0.0 63.1 jit_solution(13951827333900226100)
XLA Ops:
  0.0 1.1 %own_model.1 = (f32[4,16,4,128]{3,2,1,0:T(4,128)S(1)}, f32[1,128,128]{2,1,0:T(8,128)S(1)}, f32[1,128,128]{2,1,0:T(8,128)S(1)}) custom-call(s32[1]{0:T(128)} %bitcast.me_ref, f32[4,4]{1,0:T(4,128)} %class_factors.1, s32[16,64,128]{2,1,0:T(8,128)} %classes_hbm.1, f32[4,16,4,128]{3,2,1,0:T(4,128)} %material_hbm.1), custom_call_target="tpu_custom_call" | custom-call | flops 327680 | bytes 131072 | tf_op jit(solution)/shard_map/own_model/pallas_call | solution.py:88
  1.2 4.1 %collective-permute-start = (f32[1,128,128]{2,1,0:T(8,128)S(1)}, f32[1,128,128]{2,1,0:T(8,128)S(1)}, u32[]{:S(2)}, u32[]{:S(2)}) collective-permute-start(f32[1,128,128]{2,1,0:T(8,128)S(1)} %get-tuple-element.48.a_ref), channel_id=1, source_target_pairs={{0,8},{1,9},{2,10},{3,11},{4,12},{5,13},{6,14},{7,15},{8,0},{9,1},... | collective-permute-start | bytes 196616 | tf_op jit(solution)/shard_map/ppermute | solution.py:533
  5.3 1.5 %collective-permute-start.3 = (f32[1,128,128]{2,1,0:T(8,128)S(1)}, f32[1,128,128]{2,1,0:T(8,128)S(1)}, u32[]{:S(2)}, u32[]{:S(2)}) collective-permute-start(f32[1,128,128]{2,1,0:T(8,128)S(1)} %get-tuple-element.49.a_ref), channel_id=1, source_target_pairs={{0,2},{1,3},{2,0},{3,1},{4,6},{5,7},{6,4},{7,5},{8,10},{9,11},{10,... | collective-permute-start | bytes 196616 | tf_op jit(solution)/shard_map/ppermute | solution.py:533
  6.8 2.1 %collective-permute-done.b_ref = f32[1,128,128]{2,1,0:T(8,128)S(1)} collective-permute-done((f32[1,128,128]{2,1,0:T(8,128)S(1)}, f32[1,128,128]{2,1,0:T(8,128)S(1)}, u32[]{:S(2)}, u32[]{:S(2)}) %collective-permute-start) | collective-permute-done | bytes 65568 | tf_op jit(solution)/shard_map/ppermute | solution.py:533
  8.9 0.6 %collective-permute-start.1 = (f32[2,128,128]{2,1,0:T(8,128)S(1)}, f32[2,128,128]{2,1,0:T(8,128)S(1)}, u32[]{:S(2)}, u32[]{:S(2)}) collective-permute-start(f32[2,128,128]{2,1,0:T(8,128)S(1)} %join.6.a_ref), channel_id=1, source_target_pairs={{0,4},{1,5},{2,6},{3,7},{4,0},{5,1},{6,2},{7,3},{8,12},{9,13},{10,... | collective-permute-start | bytes 393224 | tf_op jit(solution)/shard_map/ppermute | solution.py:533
  9.5 0.0 collective-permute-done.3.b_ref
  9.6 3.4 %collective-permute-start.4 = (f32[2,128,128]{2,1,0:T(8,128)S(1)}, f32[2,128,128]{2,1,0:T(8,128)S(1)}, u32[]{:S(2)}, u32[]{:S(2)}) collective-permute-start(f32[2,128,128]{2,1,0:T(8,128)S(1)} %join.8.a_ref), channel_id=1, source_target_pairs={{0,8},{1,9},{2,10},{3,11},{4,12},{5,13},{6,14},{7,15},{8,0},{9,1},... | collective-permute-start | bytes 393224 | tf_op jit(solution)/shard_map/ppermute | solution.py:533
  13.0 3.0 %collective-permute-done.1.b_ref = f32[2,128,128]{2,1,0:T(8,128)S(1)} collective-permute-done((f32[2,128,128]{2,1,0:T(8,128)S(1)}, f32[2,128,128]{2,1,0:T(8,128)S(1)}, u32[]{:S(2)}, u32[]{:S(2)}) %collective-permute-start.1) | collective-permute-done | bytes 131104 | tf_op jit(solution)/shard_map/ppermute | solution.py:533
  16.0 2.0 %collective-permute-start.2 = (f32[4,128,128]{2,1,0:T(8,128)S(1)}, f32[4,128,128]{2,1,0:T(8,128)S(1)}, u32[]{:S(2)}, u32[]{:S(2)}) collective-permute-start(f32[4,128,128]{2,1,0:T(8,128)S(1)} %join.7.refs_0_.a_ref), channel_id=1, source_target_pairs={{0,2},{1,3},{2,0},{3,1},{4,6},{5,7},{6,4},{7,5},{8,10},{9,11},{10,... | collective-permute-start | bytes 786440 | tf_op jit(solution)/shard_map/ppermute | solution.py:533
  18.0 0.9 %collective-permute-done.4.b_ref = f32[2,128,128]{2,1,0:T(8,128)S(1)} collective-permute-done((f32[2,128,128]{2,1,0:T(8,128)S(1)}, f32[2,128,128]{2,1,0:T(8,128)S(1)}, u32[]{:S(2)}, u32[]{:S(2)}) %collective-permute-start.4) | collective-permute-done | bytes 131104 | tf_op jit(solution)/shard_map/ppermute | solution.py:533
  18.9 0.3 collective-permute-start.6
  19.9 5.4 %load_fields.1 = (f32[13,18,80,128]{3,2,1,0:T(8,128)S(1)}, f32[3,18,80,128]{3,2,1,0:T(8,128)S(1)}, f32[3,18,80,128]{3,2,1,0:T(8,128)S(1)}, f32[7,18,80,128]{3,2,...) custom-call(s32[1]{0:T(128)S(6)} %copy.58.src_cell, ...), custom_call_target="tpu_custom_call" | custom-call | flops 19660800 | bytes 524288 | tf_op jit(solution)/shard_map/load_fields/pallas_call | solution.py:196
  25.3 0.0 collective-permute-done.2.b_ref
  25.4 0.1 collective-permute-start.5
  25.5 0.0 collective-permute-done.6.b_ref
  25.5 0.5 collective-permute-start.7
  26.1 1.3 %collective-permute-done.5.refs_1_ = f32[8,128,128]{2,1,0:T(8,128)S(1)} collective-permute-done((f32[8,128,128]{2,1,0:T(8,128)S(1)}, f32[8,128,128]{2,1,0:T(8,128)S(1)}, u32[]{:S(2)}, u32[]{:S(2)}) %collective-permute-start.5) | collective-permute-done | bytes 524320 | tf_op jit(solution)/shard_map/ppermute | solution.py:533
  27.4 0.7 %collective-permute-done.7.refs_3_ = f32[8,128,128]{2,1,0:T(8,128)S(1)} collective-permute-done((f32[8,128,128]{2,1,0:T(8,128)S(1)}, f32[8,128,128]{2,1,0:T(8,128)S(1)}, u32[]{:S(2)}, u32[]{:S(2)}) %collective-permute-start.7) | collective-permute-done | bytes 524320 | tf_op jit(solution)/shard_map/ppermute | solution.py:533
  28.1 8.3 %march.2 = (f32[13,18,80,128]{3,2,1,0:T(8,128)S(1)}, f32[3,18,80,128]{3,2,1,0:T(8,128)S(1)}, f32[3,18,80,128]{3,2,1,0:T(8,128)S(1)}, f32[7,18,80,128]{3,2,1,0:T(...) custom-call(s32[1]{0:T(128)} %bitcast.me_ref, ...), custom_call_target="tpu_custom_call", output_to_operand_aliasing={{0}: (5, {}), {1}: (6, {}), {2}: (7, {}), {3}: (8, {}), {4}... | custom-call | flops 74547200 | bytes 2981888 | tf_op jit(solution)/shard_map/march/pallas_call | solution.py:457
  36.4 0.2 collective-permute-start.8
  36.6 1.9 %march.3 = (f32[13,18,80,128]{3,2,1,0:T(8,128)S(1)}, f32[3,18,80,128]{3,2,1,0:T(8,128)S(1)}, f32[3,18,80,128]{3,2,1,0:T(8,128)S(1)}, f32[7,18,80,128]{3,2,1,0:T(...) custom-call(s32[1]{0:T(128)} %bitcast.me_ref, ...), custom_call_target="tpu_custom_call", output_to_operand_aliasing={{0}: (1, {}), {1}: (2, {}), {2}: (3, {}), {3}: (4, {}), {4}... | custom-call | flops 17203200 | bytes 688128 | tf_op jit(solution)/shard_map/march/pallas_call | solution.py:457
  38.5 0.4 collective-permute-start.12
  39.0 0.0 collective-permute-done.8.b
  39.0 0.1 add_halves.6
  39.0 1.6 %collective-permute-start.9 = (f32[4,160,128]{2,1,0:T(8,128)S(1)}, f32[4,160,128]{2,1,0:T(8,128)S(1)}, u32[]{:S(2)}, u32[]{:S(2)}) collective-permute-start(f32[4,160,128]{2,1,0:T(8,128)S(1)} %get-tuple-element.65), channel_id=1, source_target_pairs={{0,2},{1,3},{2,0},{3,1},{4,6},{5,7},{6,4},{7,5},{8,10},{9,11},{10,... | collective-permute-start | bytes 983048 | tf_op jit(solution)/shard_map/ppermute | solution.py:533
  40.6 0.0 collective-permute-done.12.b
  40.7 1.9 %collective-permute-start.13 = (f32[4,96,128]{2,1,0:T(8,128)S(1)}, f32[4,96,128]{2,1,0:T(8,128)S(1)}, u32[]{:S(2)}, u32[]{:S(2)}) collective-permute-start(f32[4,96,128]{2,1,0:T(8,128)S(1)} %get-tuple-element.85), channel_id=1, source_target_pairs={{0,4},{1,5},{2,6},{3,7},{4,0},{5,1},{6,2},{7,3},{8,12},{9,13},{10,... | collective-permute-start | bytes 589832 | tf_op jit(solution)/shard_map/ppermute | solution.py:533
  42.5 6.3 %collective-permute-done.9.b = f32[4,160,128]{2,1,0:T(8,128)S(1)} collective-permute-done((f32[4,160,128]{2,1,0:T(8,128)S(1)}, f32[4,160,128]{2,1,0:T(8,128)S(1)}, u32[]{:S(2)}, u32[]{:S(2)}) %collective-permute-start.9) | collective-permute-done | bytes 327712 | tf_op jit(solution)/shard_map/ppermute | solution.py:533
  48.9 1.9 %collective-permute-start.10 = (f32[2,160,128]{2,1,0:T(8,128)S(1)}, f32[2,160,128]{2,1,0:T(8,128)S(1)}, u32[]{:S(2)}, u32[]{:S(2)}) collective-permute-start(f32[2,160,128]{2,1,0:T(8,128)S(1)} %get-tuple-element.67), channel_id=1, source_target_pairs={{0,4},{1,5},{2,6},{3,7},{4,0},{5,1},{6,2},{7,3},{8,12},{9,13},{10,... | collective-permute-start | bytes 491528 | tf_op jit(solution)/shard_map/ppermute | solution.py:533
  50.8 0.0 collective-permute-done.13.b
  50.8 1.2 %collective-permute-start.14 = (f32[2,96,128]{2,1,0:T(8,128)S(1)}, f32[2,96,128]{2,1,0:T(8,128)S(1)}, u32[]{:S(2)}, u32[]{:S(2)}) collective-permute-start(f32[2,96,128]{2,1,0:T(8,128)S(1)} %get-tuple-element.87), channel_id=1, source_target_pairs={{0,8},{1,9},{2,10},{3,11},{4,12},{5,13},{6,14},{7,15},{8,0},{9,1},... | collective-permute-start | bytes 294920 | tf_op jit(solution)/shard_map/ppermute | solution.py:533
  52.0 3.7 %collective-permute-done.10.b = f32[2,160,128]{2,1,0:T(8,128)S(1)} collective-permute-done((f32[2,160,128]{2,1,0:T(8,128)S(1)}, f32[2,160,128]{2,1,0:T(8,128)S(1)}, u32[]{:S(2)}, u32[]{:S(2)}) %collective-permute-start.10) | collective-permute-done | bytes 163872 | tf_op jit(solution)/shard_map/ppermute | solution.py:533
  55.7 2.6 %collective-permute-start.11 = (f32[1,160,128]{2,1,0:T(8,128)S(1)}, f32[1,160,128]{2,1,0:T(8,128)S(1)}, u32[]{:S(2)}, u32[]{:S(2)}) collective-permute-start(f32[1,160,128]{2,1,0:T(8,128)S(1)} %get-tuple-element.69), channel_id=1, source_target_pairs={{0,8},{1,9},{2,10},{3,11},{4,12},{5,13},{6,14},{7,15},{8,0},{9,1},... | collective-permute-start | bytes 245768 | tf_op jit(solution)/shard_map/ppermute | solution.py:533
  58.2 0.0 collective-permute-done.14.b
  58.2 1.6 %collective-permute-start.15 = (f32[1,96,128]{2,1,0:T(8,128)S(1)}, f32[1,96,128]{2,1,0:T(8,128)S(1)}, u32[]{:S(2)}, u32[]{:S(2)}) collective-permute-start(f32[1,96,128]{2,1,0:T(8,128)S(1)} %get-tuple-element.89), channel_id=1, source_target_pairs={{0,2},{1,3},{2,0},{3,1},{4,6},{5,7},{6,4},{7,5},{8,10},{9,11},{10,... | collective-permute-start | bytes 147464 | tf_op jit(solution)/shard_map/ppermute | solution.py:533
  59.8 2.6 %collective-permute-done.15.refs_3_ = f32[1,96,128]{2,1,0:T(8,128)S(1)} collective-permute-done((f32[1,96,128]{2,1,0:T(8,128)S(1)}, f32[1,96,128]{2,1,0:T(8,128)S(1)}, u32[]{:S(2)}, u32[]{:S(2)}) %collective-permute-start.15) | collective-permute-done | bytes 49184 | tf_op jit(solution)/shard_map/ppermute | solution.py:533
  62.4 0.0 collective-permute-done.11.refs_1_
  62.4 0.7 %finish.1 = f32[4,16,4,128]{3,2,1,0:T(4,128)} custom-call(f32[1,160,128]{2,1,0:T(8,128)S(1)} %get-tuple-element.68.refs_0_, f32[1,160,128]{2,1,0:T(8,128)S(1)} %collective-permute-done.11.refs_1_, f32[1,96,128]{2,1,0:T(8,128)S(1)} %get-tuple-element.88.refs_2_, f32[1,96,128]{2,1,0:T(8,128)S(1)} %collective-permute-done.15.refs_3_, ...), custom_call_target="tpu_custom_call" | custom-call | tf_op jit(solution)/shard_map/finish/pallas_call | solution.py:522
  (11 shorter events, 0.3 us)
Async XLA Ops:
  1.2 7.8 %collective-permute-start = (f32[1,128,128]{2,1,0:T(8,128)S(1)}, f32[1,128,128]{2,1,0:T(8,128)S(1)}, u32[]{:S(2)}, u32[]{:S(2)}) collective-permute-start(f32[1,128,128]{2,1,0:T(8,128)S(1)} %get-tuple-element.48.a_ref), channel_id=1, source_target_pairs={{0,8},{1,9},{2,10},{3,11},{4,12},{5,13},{6,14},{7,15},{8,0},{9,1},... | collective-permute-start | bytes 196616 | tf_op jit(solution)/shard_map/ppermute | solution.py:533
  5.3 4.3 %collective-permute-start.3 = (f32[1,128,128]{2,1,0:T(8,128)S(1)}, f32[1,128,128]{2,1,0:T(8,128)S(1)}, u32[]{:S(2)}, u32[]{:S(2)}) collective-permute-start(f32[1,128,128]{2,1,0:T(8,128)S(1)} %get-tuple-element.49.a_ref), channel_id=1, source_target_pairs={{0,2},{1,3},{2,0},{3,1},{4,6},{5,7},{6,4},{7,5},{8,10},{9,11},{10,... | collective-permute-start | bytes 196616 | tf_op jit(solution)/shard_map/ppermute | solution.py:533
  8.9 7.1 %collective-permute-start.1 = (f32[2,128,128]{2,1,0:T(8,128)S(1)}, f32[2,128,128]{2,1,0:T(8,128)S(1)}, u32[]{:S(2)}, u32[]{:S(2)}) collective-permute-start(f32[2,128,128]{2,1,0:T(8,128)S(1)} %join.6.a_ref), channel_id=1, source_target_pairs={{0,4},{1,5},{2,6},{3,7},{4,0},{5,1},{6,2},{7,3},{8,12},{9,13},{10,... | collective-permute-start | bytes 393224 | tf_op jit(solution)/shard_map/ppermute | solution.py:533
  9.6 9.3 %collective-permute-start.4 = (f32[2,128,128]{2,1,0:T(8,128)S(1)}, f32[2,128,128]{2,1,0:T(8,128)S(1)}, u32[]{:S(2)}, u32[]{:S(2)}) collective-permute-start(f32[2,128,128]{2,1,0:T(8,128)S(1)} %join.8.a_ref), channel_id=1, source_target_pairs={{0,8},{1,9},{2,10},{3,11},{4,12},{5,13},{6,14},{7,15},{8,0},{9,1},... | collective-permute-start | bytes 393224 | tf_op jit(solution)/shard_map/ppermute | solution.py:533
  16.0 9.3 %collective-permute-start.2 = (f32[4,128,128]{2,1,0:T(8,128)S(1)}, f32[4,128,128]{2,1,0:T(8,128)S(1)}, u32[]{:S(2)}, u32[]{:S(2)}) collective-permute-start(f32[4,128,128]{2,1,0:T(8,128)S(1)} %join.7.refs_0_.a_ref), channel_id=1, source_target_pairs={{0,2},{1,3},{2,0},{3,1},{4,6},{5,7},{6,4},{7,5},{8,10},{9,11},{10,... | collective-permute-start | bytes 786440 | tf_op jit(solution)/shard_map/ppermute | solution.py:533
  18.9 6.5 %collective-permute-start.6 = (f32[4,128,128]{2,1,0:T(8,128)S(1)}, f32[4,128,128]{2,1,0:T(8,128)S(1)}, u32[]{:S(2)}, u32[]{:S(2)}) collective-permute-start(f32[4,128,128]{2,1,0:T(8,128)S(1)} %join.9.refs_1_.a_ref), channel_id=1, source_target_pairs={{0,4},{1,5},{2,6},{3,7},{4,0},{5,1},{6,2},{7,3},{8,12},{9,13},{10,... | collective-permute-start | bytes 786440 | tf_op jit(solution)/shard_map/ppermute | solution.py:533
  25.4 2.0 %collective-permute-start.5 = (f32[8,128,128]{2,1,0:T(8,128)S(1)}, f32[8,128,128]{2,1,0:T(8,128)S(1)}, u32[]{:S(2)}, u32[]{:S(2)}) collective-permute-start(f32[8,128,128]{2,1,0:T(8,128)S(1)} %join.10.refs_0_), channel_id=1, source_target_pairs={{0,1},{1,0},{2,3},{3,2},{4,5},{5,4},{6,7},{7,6},{8,9},{9,8},{10,11... | collective-permute-start | bytes 1572872 | tf_op jit(solution)/shard_map/ppermute | solution.py:533
  25.5 2.6 %collective-permute-start.7 = (f32[8,128,128]{2,1,0:T(8,128)S(1)}, f32[8,128,128]{2,1,0:T(8,128)S(1)}, u32[]{:S(2)}, u32[]{:S(2)}) collective-permute-start(f32[8,128,128]{2,1,0:T(8,128)S(1)} %join.11.refs_2_), channel_id=1, source_target_pairs={{0,1},{1,0},{2,3},{3,2},{4,5},{5,4},{6,7},{7,6},{8,9},{9,8},{10,11... | collective-permute-start | bytes 1572872 | tf_op jit(solution)/shard_map/ppermute | solution.py:533
  36.4 2.6 %collective-permute-start.8 = (f32[8,160,128]{2,1,0:T(8,128)S(1)}, f32[8,160,128]{2,1,0:T(8,128)S(1)}, u32[]{:S(2)}, u32[]{:S(2)}) collective-permute-start(f32[8,160,128]{2,1,0:T(8,128)S(1)} %get-tuple-element.63), channel_id=1, source_target_pairs={{0,1},{1,0},{2,3},{3,2},{4,5},{5,4},{6,7},{7,6},{8,9},{9,8},{10,11... | collective-permute-start | bytes 1966088 | tf_op jit(solution)/shard_map/ppermute | solution.py:533
  38.5 2.1 %collective-permute-start.12 = (f32[8,96,128]{2,1,0:T(8,128)S(1)}, f32[8,96,128]{2,1,0:T(8,128)S(1)}, u32[]{:S(2)}, u32[]{:S(2)}) collective-permute-start(f32[8,96,128]{2,1,0:T(8,128)S(1)} %get-tuple-element.83), channel_id=1, source_target_pairs={{0,1},{1,0},{2,3},{3,2},{4,5},{5,4},{6,7},{7,6},{8,9},{9,8},{10,11... | collective-permute-start | bytes 1179656 | tf_op jit(solution)/shard_map/ppermute | solution.py:533
  39.0 9.8 %collective-permute-start.9 = (f32[4,160,128]{2,1,0:T(8,128)S(1)}, f32[4,160,128]{2,1,0:T(8,128)S(1)}, u32[]{:S(2)}, u32[]{:S(2)}) collective-permute-start(f32[4,160,128]{2,1,0:T(8,128)S(1)} %get-tuple-element.65), channel_id=1, source_target_pairs={{0,2},{1,3},{2,0},{3,1},{4,6},{5,7},{6,4},{7,5},{8,10},{9,11},{10,... | collective-permute-start | bytes 983048 | tf_op jit(solution)/shard_map/ppermute | solution.py:533
  40.7 10.1 %collective-permute-start.13 = (f32[4,96,128]{2,1,0:T(8,128)S(1)}, f32[4,96,128]{2,1,0:T(8,128)S(1)}, u32[]{:S(2)}, u32[]{:S(2)}) collective-permute-start(f32[4,96,128]{2,1,0:T(8,128)S(1)} %get-tuple-element.85), channel_id=1, source_target_pairs={{0,4},{1,5},{2,6},{3,7},{4,0},{5,1},{6,2},{7,3},{8,12},{9,13},{10,... | collective-permute-start | bytes 589832 | tf_op jit(solution)/shard_map/ppermute | solution.py:533
  48.9 6.7 %collective-permute-start.10 = (f32[2,160,128]{2,1,0:T(8,128)S(1)}, f32[2,160,128]{2,1,0:T(8,128)S(1)}, u32[]{:S(2)}, u32[]{:S(2)}) collective-permute-start(f32[2,160,128]{2,1,0:T(8,128)S(1)} %get-tuple-element.67), channel_id=1, source_target_pairs={{0,4},{1,5},{2,6},{3,7},{4,0},{5,1},{6,2},{7,3},{8,12},{9,13},{10,... | collective-permute-start | bytes 491528 | tf_op jit(solution)/shard_map/ppermute | solution.py:533
  50.8 7.4 %collective-permute-start.14 = (f32[2,96,128]{2,1,0:T(8,128)S(1)}, f32[2,96,128]{2,1,0:T(8,128)S(1)}, u32[]{:S(2)}, u32[]{:S(2)}) collective-permute-start(f32[2,96,128]{2,1,0:T(8,128)S(1)} %get-tuple-element.87), channel_id=1, source_target_pairs={{0,8},{1,9},{2,10},{3,11},{4,12},{5,13},{6,14},{7,15},{8,0},{9,1},... | collective-permute-start | bytes 294920 | tf_op jit(solution)/shard_map/ppermute | solution.py:533
  55.7 6.7 %collective-permute-start.11 = (f32[1,160,128]{2,1,0:T(8,128)S(1)}, f32[1,160,128]{2,1,0:T(8,128)S(1)}, u32[]{:S(2)}, u32[]{:S(2)}) collective-permute-start(f32[1,160,128]{2,1,0:T(8,128)S(1)} %get-tuple-element.69), channel_id=1, source_target_pairs={{0,8},{1,9},{2,10},{3,11},{4,12},{5,13},{6,14},{7,15},{8,0},{9,1},... | collective-permute-start | bytes 245768 | tf_op jit(solution)/shard_map/ppermute | solution.py:533
  58.2 4.2 %collective-permute-start.15 = (f32[1,96,128]{2,1,0:T(8,128)S(1)}, f32[1,96,128]{2,1,0:T(8,128)S(1)}, u32[]{:S(2)}, u32[]{:S(2)}) collective-permute-start(f32[1,96,128]{2,1,0:T(8,128)S(1)} %get-tuple-element.89), channel_id=1, source_target_pairs={{0,2},{1,3},{2,0},{3,1},{4,6},{5,7},{6,4},{7,5},{8,10},{9,11},{10,... | collective-permute-start | bytes 147464 | tf_op jit(solution)/shard_map/ppermute | solution.py:533

commit v2 on v1

--- a/solution.py
+++ b/solution.py
@@ -553,7 +553,7 @@
     along_z = [b for b in (4, 8, 16, 32, 64, 128) if b < n]
 
     factor, *owns = own_model(me, class_factors, cell_class, material, 2)
-    ways = ([*along_z[::-1], 2], [2, *along_z[::-1]])
+    ways = ([2, *along_z[::-1]], [*along_z[::-1], 2])
     data, rels = list(owns), [[0], [0]]
     fields, token = None, ()
     for step in range(len(ways[0])):

time: 63.3 us -> 62.1 us (0.981)
  waiting for transfers between devices: 20.7 us -> 19.5 us
    ppermute x16, waiting for transfers between devices: 20.7 us -> 19.5 us  [partner(): return lax.ppermute(x, 'shot', [(i, i ^ bit) for i in range(n)])]
  transfers between devices with their start and end apart: 16 -> 16, of which waited for: 8 -> 10; matrix products, arithmetic and copies ran while one was open for 0% -> 0% of each run, Pallas kernels for 12% -> 12%
where the time goes in v2:
time: 62.1 us; the launch traced here: 62 us
  starting transfers between devices  23.9 us (38%)
  waiting for transfers between devices  19.5 us (31%)
  Pallas kernels  17.8 us (29%)
  between operations  0.76 us (1%)
    ppermute x16, starting transfers between devices, partner(): return lax.ppermute(x, 'shot', [(i, i ^ bit) for i in range(n)])  23.9 us
    ppermute x16, waiting for transfers between devices, partner(): return lax.ppermute(x, 'shot', [(i, i ^ bit) for i in range(n)])  19.5 us
    pallas_call x2, Pallas kernels, march(): pl.pallas_call(functools.partial(march_kernel, n=n, spans=spans, gathered...  10.2 us
    pallas_call x1, Pallas kernels, load_fields(): pl.pallas_call(functools.partial(load_kernel, waits=len(after)), out_shap...  5.44 us
  transfers between devices with their start and end apart: 16, of which 10 were waited for; matrix products, arithmetic and copies ran while one was open for 0% of the time, Pallas kernels for 12%

profile of v2, /device:TPU:0, one launch (start us, length us, event | category | flops | bytes accessed | tf_op | source)
XLA Modules:
  0.0 62.0 jit_solution(11214129200096487283)
XLA Ops:
  0.0 1.1 %own_model.1 = (f32[4,16,4,128]{3,2,1,0:T(4,128)S(1)}, f32[1,128,128]{2,1,0:T(8,128)S(1)}, f32[1,128,128]{2,1,0:T(8,128)S(1)}) custom-call(s32[1]{0:T(128)} %bitcast.me_ref, f32[4,4]{1,0:T(4,128)} %class_factors.1, s32[16,64,128]{2,1,0:T(8,128)} %classes_hbm.1, f32[4,16,4,128]{3,2,1,0:T(4,128)} %material_hbm.1), custom_call_target="tpu_custom_call" | custom-call | flops 327680 | bytes 131072 | tf_op jit(solution)/shard_map/own_model/pallas_call | solution.py:88
  1.2 3.0 %collective-permute-start = (f32[1,128,128]{2,1,0:T(8,128)S(1)}, f32[1,128,128]{2,1,0:T(8,128)S(1)}, u32[]{:S(2)}, u32[]{:S(2)}) collective-permute-start(f32[1,128,128]{2,1,0:T(8,128)S(1)} %get-tuple-element.48.a_ref), channel_id=1, source_target_pairs={{0,2},{1,3},{2,0},{3,1},{4,6},{5,7},{6,4},{7,5},{8,10},{9,11},{10,... | collective-permute-start | bytes 196616 | tf_op jit(solution)/shard_map/ppermute | solution.py:533
  4.2 2.6 %collective-permute-start.3 = (f32[1,128,128]{2,1,0:T(8,128)S(1)}, f32[1,128,128]{2,1,0:T(8,128)S(1)}, u32[]{:S(2)}, u32[]{:S(2)}) collective-permute-start(f32[1,128,128]{2,1,0:T(8,128)S(1)} %get-tuple-element.49.a_ref), channel_id=1, source_target_pairs={{0,8},{1,9},{2,10},{3,11},{4,12},{5,13},{6,14},{7,15},{8,0},{9,1},... | collective-permute-start | bytes 196616 | tf_op jit(solution)/shard_map/ppermute | solution.py:533
  6.8 0.0 collective-permute-done.b_ref
  6.8 2.8 %collective-permute-start.1 = (f32[2,128,128]{2,1,0:T(8,128)S(1)}, f32[2,128,128]{2,1,0:T(8,128)S(1)}, u32[]{:S(2)}, u32[]{:S(2)}) collective-permute-start(f32[2,128,128]{2,1,0:T(8,128)S(1)} %join.6.a_ref), channel_id=1, source_target_pairs={{0,8},{1,9},{2,10},{3,11},{4,12},{5,13},{6,14},{7,15},{8,0},{9,1},... | collective-permute-start | bytes 393224 | tf_op jit(solution)/shard_map/ppermute | solution.py:533
  9.6 0.1 collective-permute-done.3.b_ref
  9.7 3.2 %collective-permute-start.4 = (f32[2,128,128]{2,1,0:T(8,128)S(1)}, f32[2,128,128]{2,1,0:T(8,128)S(1)}, u32[]{:S(2)}, u32[]{:S(2)}) collective-permute-start(f32[2,128,128]{2,1,0:T(8,128)S(1)} %join.8.a_ref), channel_id=1, source_target_pairs={{0,4},{1,5},{2,6},{3,7},{4,0},{5,1},{6,2},{7,3},{8,12},{9,13},{10,... | collective-permute-start | bytes 393224 | tf_op jit(solution)/shard_map/ppermute | solution.py:533
  12.9 3.1 %collective-permute-done.1.b_ref = f32[2,128,128]{2,1,0:T(8,128)S(1)} collective-permute-done((f32[2,128,128]{2,1,0:T(8,128)S(1)}, f32[2,128,128]{2,1,0:T(8,128)S(1)}, u32[]{:S(2)}, u32[]{:S(2)}) %collective-permute-start.1) | collective-permute-done | bytes 131104 | tf_op jit(solution)/shard_map/ppermute | solution.py:533
  16.1 0.4 collective-permute-start.2
  16.4 0.7 %collective-permute-done.4.b_ref = f32[2,128,128]{2,1,0:T(8,128)S(1)} collective-permute-done((f32[2,128,128]{2,1,0:T(8,128)S(1)}, f32[2,128,128]{2,1,0:T(8,128)S(1)}, u32[]{:S(2)}, u32[]{:S(2)}) %collective-permute-start.4) | collective-permute-done | bytes 131104 | tf_op jit(solution)/shard_map/ppermute | solution.py:533
  17.1 0.1 collective-permute-start.6
  17.9 5.4 %load_fields.1 = (f32[13,18,80,128]{3,2,1,0:T(8,128)S(1)}, f32[3,18,80,128]{3,2,1,0:T(8,128)S(1)}, f32[3,18,80,128]{3,2,1,0:T(8,128)S(1)}, f32[7,18,80,128]{3,2,...) custom-call(s32[1]{0:T(128)S(6)} %copy.58.src_cell, ...), custom_call_target="tpu_custom_call" | custom-call | flops 19660800 | bytes 524288 | tf_op jit(solution)/shard_map/load_fields/pallas_call | solution.py:196
  23.3 0.8 %collective-permute-done.2.b_ref = f32[4,128,128]{2,1,0:T(8,128)S(1)} collective-permute-done((f32[4,128,128]{2,1,0:T(8,128)S(1)}, f32[4,128,128]{2,1,0:T(8,128)S(1)}, u32[]{:S(2)}, u32[]{:S(2)}) %collective-permute-start.2) | collective-permute-done | bytes 262176 | tf_op jit(solution)/shard_map/ppermute | solution.py:533
  24.1 0.1 collective-permute-start.5
  24.2 0.0 collective-permute-done.6.b_ref
  24.3 0.5 collective-permute-start.7
  24.8 1.3 %collective-permute-done.5.refs_1_ = f32[8,128,128]{2,1,0:T(8,128)S(1)} collective-permute-done((f32[8,128,128]{2,1,0:T(8,128)S(1)}, f32[8,128,128]{2,1,0:T(8,128)S(1)}, u32[]{:S(2)}, u32[]{:S(2)}) %collective-permute-start.5) | collective-permute-done | bytes 524320 | tf_op jit(solution)/shard_map/ppermute | solution.py:533
  26.1 0.7 %collective-permute-done.7.refs_3_ = f32[8,128,128]{2,1,0:T(8,128)S(1)} collective-permute-done((f32[8,128,128]{2,1,0:T(8,128)S(1)}, f32[8,128,128]{2,1,0:T(8,128)S(1)}, u32[]{:S(2)}, u32[]{:S(2)}) %collective-permute-start.7) | collective-permute-done | bytes 524320 | tf_op jit(solution)/shard_map/ppermute | solution.py:533
  26.9 8.3 %march.2 = (f32[13,18,80,128]{3,2,1,0:T(8,128)S(1)}, f32[3,18,80,128]{3,2,1,0:T(8,128)S(1)}, f32[3,18,80,128]{3,2,1,0:T(8,128)S(1)}, f32[7,18,80,128]{3,2,1,0:T(...) custom-call(s32[1]{0:T(128)} %bitcast.me_ref, ...), custom_call_target="tpu_custom_call", output_to_operand_aliasing={{0}: (5, {}), {1}: (6, {}), {2}: (7, {}), {3}: (8, {}), {4}... | custom-call | flops 74547200 | bytes 2981888 | tf_op jit(solution)/shard_map/march/pallas_call | solution.py:457
  35.2 0.2 collective-permute-start.8
  35.4 1.9 %march.3 = (f32[13,18,80,128]{3,2,1,0:T(8,128)S(1)}, f32[3,18,80,128]{3,2,1,0:T(8,128)S(1)}, f32[3,18,80,128]{3,2,1,0:T(8,128)S(1)}, f32[7,18,80,128]{3,2,1,0:T(...) custom-call(s32[1]{0:T(128)} %bitcast.me_ref, ...), custom_call_target="tpu_custom_call", output_to_operand_aliasing={{0}: (1, {}), {1}: (2, {}), {2}: (3, {}), {3}: (4, {}), {4}... | custom-call | flops 17203200 | bytes 688128 | tf_op jit(solution)/shard_map/march/pallas_call | solution.py:457
  37.3 0.4 collective-permute-start.12
  37.7 0.0 collective-permute-done.8.b
  37.7 0.1 add_halves.6
  37.8 1.3 %collective-permute-start.9 = (f32[4,160,128]{2,1,0:T(8,128)S(1)}, f32[4,160,128]{2,1,0:T(8,128)S(1)}, u32[]{:S(2)}, u32[]{:S(2)}) collective-permute-start(f32[4,160,128]{2,1,0:T(8,128)S(1)} %get-tuple-element.65), channel_id=1, source_target_pairs={{0,2},{1,3},{2,0},{3,1},{4,6},{5,7},{6,4},{7,5},{8,10},{9,11},{10,... | collective-permute-start | bytes 983048 | tf_op jit(solution)/shard_map/ppermute | solution.py:533
  39.1 0.0 collective-permute-done.12.b
  39.1 1.1 %collective-permute-start.13 = (f32[4,96,128]{2,1,0:T(8,128)S(1)}, f32[4,96,128]{2,1,0:T(8,128)S(1)}, u32[]{:S(2)}, u32[]{:S(2)}) collective-permute-start(f32[4,96,128]{2,1,0:T(8,128)S(1)} %get-tuple-element.85), channel_id=1, source_target_pairs={{0,4},{1,5},{2,6},{3,7},{4,0},{5,1},{6,2},{7,3},{8,12},{9,13},{10,... | collective-permute-start | bytes 589832 | tf_op jit(solution)/shard_map/ppermute | solution.py:533
  40.3 7.3 %collective-permute-done.9.b = f32[4,160,128]{2,1,0:T(8,128)S(1)} collective-permute-done((f32[4,160,128]{2,1,0:T(8,128)S(1)}, f32[4,160,128]{2,1,0:T(8,128)S(1)}, u32[]{:S(2)}, u32[]{:S(2)}) %collective-permute-start.9) | collective-permute-done | bytes 327712 | tf_op jit(solution)/shard_map/ppermute | solution.py:533
  47.6 1.2 %collective-permute-start.10 = (f32[2,160,128]{2,1,0:T(8,128)S(1)}, f32[2,160,128]{2,1,0:T(8,128)S(1)}, u32[]{:S(2)}, u32[]{:S(2)}) collective-permute-start(f32[2,160,128]{2,1,0:T(8,128)S(1)} %get-tuple-element.67), channel_id=1, source_target_pairs={{0,4},{1,5},{2,6},{3,7},{4,0},{5,1},{6,2},{7,3},{8,12},{9,13},{10,... | collective-permute-start | bytes 491528 | tf_op jit(solution)/shard_map/ppermute | solution.py:533
  48.8 0.0 collective-permute-done.13.b
  48.8 3.1 %collective-permute-start.14 = (f32[2,96,128]{2,1,0:T(8,128)S(1)}, f32[2,96,128]{2,1,0:T(8,128)S(1)}, u32[]{:S(2)}, u32[]{:S(2)}) collective-permute-start(f32[2,96,128]{2,1,0:T(8,128)S(1)} %get-tuple-element.87), channel_id=1, source_target_pairs={{0,8},{1,9},{2,10},{3,11},{4,12},{5,13},{6,14},{7,15},{8,0},{9,1},... | collective-permute-start | bytes 294920 | tf_op jit(solution)/shard_map/ppermute | solution.py:533
  52.0 3.0 %collective-permute-done.10.b = f32[2,160,128]{2,1,0:T(8,128)S(1)} collective-permute-done((f32[2,160,128]{2,1,0:T(8,128)S(1)}, f32[2,160,128]{2,1,0:T(8,128)S(1)}, u32[]{:S(2)}, u32[]{:S(2)}) %collective-permute-start.10) | collective-permute-done | bytes 163872 | tf_op jit(solution)/shard_map/ppermute | solution.py:533
  55.0 2.0 %collective-permute-start.11 = (f32[1,160,128]{2,1,0:T(8,128)S(1)}, f32[1,160,128]{2,1,0:T(8,128)S(1)}, u32[]{:S(2)}, u32[]{:S(2)}) collective-permute-start(f32[1,160,128]{2,1,0:T(8,128)S(1)} %get-tuple-element.69), channel_id=1, source_target_pairs={{0,8},{1,9},{2,10},{3,11},{4,12},{5,13},{6,14},{7,15},{8,0},{9,1},... | collective-permute-start | bytes 245768 | tf_op jit(solution)/shard_map/ppermute | solution.py:533
  57.0 0.0 collective-permute-done.14.b
  57.0 1.7 %collective-permute-start.15 = (f32[1,96,128]{2,1,0:T(8,128)S(1)}, f32[1,96,128]{2,1,0:T(8,128)S(1)}, u32[]{:S(2)}, u32[]{:S(2)}) collective-permute-start(f32[1,96,128]{2,1,0:T(8,128)S(1)} %get-tuple-element.89), channel_id=1, source_target_pairs={{0,2},{1,3},{2,0},{3,1},{4,6},{5,7},{6,4},{7,5},{8,10},{9,11},{10,... | collective-permute-start | bytes 147464 | tf_op jit(solution)/shard_map/ppermute | solution.py:533
  58.7 2.4 %collective-permute-done.15.refs_3_ = f32[1,96,128]{2,1,0:T(8,128)S(1)} collective-permute-done((f32[1,96,128]{2,1,0:T(8,128)S(1)}, f32[1,96,128]{2,1,0:T(8,128)S(1)}, u32[]{:S(2)}, u32[]{:S(2)}) %collective-permute-start.15) | collective-permute-done | bytes 49184 | tf_op jit(solution)/shard_map/ppermute | solution.py:533
  61.2 0.1 collective-permute-done.11.refs_1_
  61.3 0.7 %finish.1 = f32[4,16,4,128]{3,2,1,0:T(4,128)} custom-call(f32[1,160,128]{2,1,0:T(8,128)S(1)} %get-tuple-element.68.refs_0_, f32[1,160,128]{2,1,0:T(8,128)S(1)} %collective-permute-done.11.refs_1_, f32[1,96,128]{2,1,0:T(8,128)S(1)} %get-tuple-element.88.refs_2_, f32[1,96,128]{2,1,0:T(8,128)S(1)} %collective-permute-done.15.refs_3_, ...), custom_call_target="tpu_custom_call" | custom-call | tf_op jit(solution)/shard_map/finish/pallas_call | solution.py:522
  (11 shorter events, 0.3 us)
Async XLA Ops:
  1.2 5.6 %collective-permute-start = (f32[1,128,128]{2,1,0:T(8,128)S(1)}, f32[1,128,128]{2,1,0:T(8,128)S(1)}, u32[]{:S(2)}, u32[]{:S(2)}) collective-permute-start(f32[1,128,128]{2,1,0:T(8,128)S(1)} %get-tuple-element.48.a_ref), channel_id=1, source_target_pairs={{0,2},{1,3},{2,0},{3,1},{4,6},{5,7},{6,4},{7,5},{8,10},{9,11},{10,... | collective-permute-start | bytes 196616 | tf_op jit(solution)/shard_map/ppermute | solution.py:533
  4.2 5.5 %collective-permute-start.3 = (f32[1,128,128]{2,1,0:T(8,128)S(1)}, f32[1,128,128]{2,1,0:T(8,128)S(1)}, u32[]{:S(2)}, u32[]{:S(2)}) collective-permute-start(f32[1,128,128]{2,1,0:T(8,128)S(1)} %get-tuple-element.49.a_ref), channel_id=1, source_target_pairs={{0,8},{1,9},{2,10},{3,11},{4,12},{5,13},{6,14},{7,15},{8,0},{9,1},... | collective-permute-start | bytes 196616 | tf_op jit(solution)/shard_map/ppermute | solution.py:533
  6.8 9.2 %collective-permute-start.1 = (f32[2,128,128]{2,1,0:T(8,128)S(1)}, f32[2,128,128]{2,1,0:T(8,128)S(1)}, u32[]{:S(2)}, u32[]{:S(2)}) collective-permute-start(f32[2,128,128]{2,1,0:T(8,128)S(1)} %join.6.a_ref), channel_id=1, source_target_pairs={{0,8},{1,9},{2,10},{3,11},{4,12},{5,13},{6,14},{7,15},{8,0},{9,1},... | collective-permute-start | bytes 393224 | tf_op jit(solution)/shard_map/ppermute | solution.py:533
  9.7 7.4 %collective-permute-start.4 = (f32[2,128,128]{2,1,0:T(8,128)S(1)}, f32[2,128,128]{2,1,0:T(8,128)S(1)}, u32[]{:S(2)}, u32[]{:S(2)}) collective-permute-start(f32[2,128,128]{2,1,0:T(8,128)S(1)} %join.8.a_ref), channel_id=1, source_target_pairs={{0,4},{1,5},{2,6},{3,7},{4,0},{5,1},{6,2},{7,3},{8,12},{9,13},{10,... | collective-permute-start | bytes 393224 | tf_op jit(solution)/shard_map/ppermute | solution.py:533
  16.1 8.0 %collective-permute-start.2 = (f32[4,128,128]{2,1,0:T(8,128)S(1)}, f32[4,128,128]{2,1,0:T(8,128)S(1)}, u32[]{:S(2)}, u32[]{:S(2)}) collective-permute-start(f32[4,128,128]{2,1,0:T(8,128)S(1)} %join.7.refs_0_.a_ref), channel_id=1, source_target_pairs={{0,4},{1,5},{2,6},{3,7},{4,0},{5,1},{6,2},{7,3},{8,12},{9,13},{10,... | collective-permute-start | bytes 786440 | tf_op jit(solution)/shard_map/ppermute | solution.py:533
  17.1 7.1 %collective-permute-start.6 = (f32[4,128,128]{2,1,0:T(8,128)S(1)}, f32[4,128,128]{2,1,0:T(8,128)S(1)}, u32[]{:S(2)}, u32[]{:S(2)}) collective-permute-start(f32[4,128,128]{2,1,0:T(8,128)S(1)} %join.9.refs_1_.a_ref), channel_id=1, source_target_pairs={{0,2},{1,3},{2,0},{3,1},{4,6},{5,7},{6,4},{7,5},{8,10},{9,11},{10,... | collective-permute-start | bytes 786440 | tf_op jit(solution)/shard_map/ppermute | solution.py:533
  24.1 2.0 %collective-permute-start.5 = (f32[8,128,128]{2,1,0:T(8,128)S(1)}, f32[8,128,128]{2,1,0:T(8,128)S(1)}, u32[]{:S(2)}, u32[]{:S(2)}) collective-permute-start(f32[8,128,128]{2,1,0:T(8,128)S(1)} %join.10.refs_0_), channel_id=1, source_target_pairs={{0,1},{1,0},{2,3},{3,2},{4,5},{5,4},{6,7},{7,6},{8,9},{9,8},{10,11... | collective-permute-start | bytes 1572872 | tf_op jit(solution)/shard_map/ppermute | solution.py:533
  24.3 2.6 %collective-permute-start.7 = (f32[8,128,128]{2,1,0:T(8,128)S(1)}, f32[8,128,128]{2,1,0:T(8,128)S(1)}, u32[]{:S(2)}, u32[]{:S(2)}) collective-permute-start(f32[8,128,128]{2,1,0:T(8,128)S(1)} %join.11.refs_2_), channel_id=1, source_target_pairs={{0,1},{1,0},{2,3},{3,2},{4,5},{5,4},{6,7},{7,6},{8,9},{9,8},{10,11... | collective-permute-start | bytes 1572872 | tf_op jit(solution)/shard_map/ppermute | solution.py:533
  35.2 2.6 %collective-permute-start.8 = (f32[8,160,128]{2,1,0:T(8,128)S(1)}, f32[8,160,128]{2,1,0:T(8,128)S(1)}, u32[]{:S(2)}, u32[]{:S(2)}) collective-permute-start(f32[8,160,128]{2,1,0:T(8,128)S(1)} %get-tuple-element.63), channel_id=1, source_target_pairs={{0,1},{1,0},{2,3},{3,2},{4,5},{5,4},{6,7},{7,6},{8,9},{9,8},{10,11... | collective-permute-start | bytes 1966088 | tf_op jit(solution)/shard_map/ppermute | solution.py:533
  37.3 1.8 %collective-permute-start.12 = (f32[8,96,128]{2,1,0:T(8,128)S(1)}, f32[8,96,128]{2,1,0:T(8,128)S(1)}, u32[]{:S(2)}, u32[]{:S(2)}) collective-permute-start(f32[8,96,128]{2,1,0:T(8,128)S(1)} %get-tuple-element.83), channel_id=1, source_target_pairs={{0,1},{1,0},{2,3},{3,2},{4,5},{5,4},{6,7},{7,6},{8,9},{9,8},{10,11... | collective-permute-start | bytes 1179656 | tf_op jit(solution)/shard_map/ppermute | solution.py:533
  37.8 9.8 %collective-permute-start.9 = (f32[4,160,128]{2,1,0:T(8,128)S(1)}, f32[4,160,128]{2,1,0:T(8,128)S(1)}, u32[]{:S(2)}, u32[]{:S(2)}) collective-permute-start(f32[4,160,128]{2,1,0:T(8,128)S(1)} %get-tuple-element.65), channel_id=1, source_target_pairs={{0,2},{1,3},{2,0},{3,1},{4,6},{5,7},{6,4},{7,5},{8,10},{9,11},{10,... | collective-permute-start | bytes 983048 | tf_op jit(solution)/shard_map/ppermute | solution.py:533
  39.1 9.7 %collective-permute-start.13 = (f32[4,96,128]{2,1,0:T(8,128)S(1)}, f32[4,96,128]{2,1,0:T(8,128)S(1)}, u32[]{:S(2)}, u32[]{:S(2)}) collective-permute-start(f32[4,96,128]{2,1,0:T(8,128)S(1)} %get-tuple-element.85), channel_id=1, source_target_pairs={{0,4},{1,5},{2,6},{3,7},{4,0},{5,1},{6,2},{7,3},{8,12},{9,13},{10,... | collective-permute-start | bytes 589832 | tf_op jit(solution)/shard_map/ppermute | solution.py:533
  47.6 7.3 %collective-permute-start.10 = (f32[2,160,128]{2,1,0:T(8,128)S(1)}, f32[2,160,128]{2,1,0:T(8,128)S(1)}, u32[]{:S(2)}, u32[]{:S(2)}) collective-permute-start(f32[2,160,128]{2,1,0:T(8,128)S(1)} %get-tuple-element.67), channel_id=1, source_target_pairs={{0,4},{1,5},{2,6},{3,7},{4,0},{5,1},{6,2},{7,3},{8,12},{9,13},{10,... | collective-permute-start | bytes 491528 | tf_op jit(solution)/shard_map/ppermute | solution.py:533
  48.8 8.2 %collective-permute-start.14 = (f32[2,96,128]{2,1,0:T(8,128)S(1)}, f32[2,96,128]{2,1,0:T(8,128)S(1)}, u32[]{:S(2)}, u32[]{:S(2)}) collective-permute-start(f32[2,96,128]{2,1,0:T(8,128)S(1)} %get-tuple-element.87), channel_id=1, source_target_pairs={{0,8},{1,9},{2,10},{3,11},{4,12},{5,13},{6,14},{7,15},{8,0},{9,1},... | collective-permute-start | bytes 294920 | tf_op jit(solution)/shard_map/ppermute | solution.py:533
  55.0 6.3 %collective-permute-start.11 = (f32[1,160,128]{2,1,0:T(8,128)S(1)}, f32[1,160,128]{2,1,0:T(8,128)S(1)}, u32[]{:S(2)}, u32[]{:S(2)}) collective-permute-start(f32[1,160,128]{2,1,0:T(8,128)S(1)} %get-tuple-element.69), channel_id=1, source_target_pairs={{0,8},{1,9},{2,10},{3,11},{4,12},{5,13},{6,14},{7,15},{8,0},{9,1},... | collective-permute-start | bytes 245768 | tf_op jit(solution)/shard_map/ppermute | solution.py:533
  57.0 4.2 %collective-permute-start.15 = (f32[1,96,128]{2,1,0:T(8,128)S(1)}, f32[1,96,128]{2,1,0:T(8,128)S(1)}, u32[]{:S(2)}, u32[]{:S(2)}) collective-permute-start(f32[1,96,128]{2,1,0:T(8,128)S(1)} %get-tuple-element.89), channel_id=1, source_target_pairs={{0,2},{1,3},{2,0},{3,1},{4,6},{5,7},{6,4},{7,5},{8,10},{9,11},{10,... | collective-permute-start | bytes 147464 | tf_op jit(solution)/shard_map/ppermute | solution.py:533
